TPU v7x, 32 devices: a whole 2x2x4 slice. The times are simulated.
32 devices in a mesh: group: 4 (over x, core), dev: 8 (over z, y).
Axes of the slice: x: 2, y: 2, z: 4, core: 2. Of those that a mesh axis runs over, the one named last changes fastest.
Arguments:
- couplings: bfloat16 [32, 6, 4, 512, 512], P(('group', 'dev')), may hold values from -0.0625 to 0.0625
- history: bfloat16 [32, 16384, 256], P(None, ('group', 'dev')), may hold values from -6 to 6
- diag_inverse: bfloat16 [32, 512, 512], P(('group', 'dev')), may hold values from -0.25 to 0.25
- incident: bfloat16 [2, 16384, 256], P(None, ('group', 'dev')), may hold values from -6 to 6
- targets: int32 [32, 6], P(('group', 'dev')), may hold values from 0 to 10
- delays: int32 [32, 6], P(('group', 'dev')), may hold values from 1 to 29
- counts: int32 [32], P(('group', 'dev')), may hold values from 1 to 6, as said below
Outputs:
- currents: bfloat16 [2, 16384, 256], P(None, ('group', 'dev'))
Inputs may be any that keep to these rules, and one draw needn't show every extreme that they name: `counts`: slots beyond a block's count carry matrices that are not couplings. Some block uses all 6 slots.
All inputs are finite; a program needn't handle non-finite values.
Results may differ from a plain program's by a relative error of at most 0.0048.
Values sent between devices are 32-bit elements; how exact they have to be, the bound alone decides.
No kernel may reach another device: no remote copies, remote signals or barrier semaphores. Data moves between devices by JAX's collectives and lax.ppermute only.
A program may use at most 128 MiB of HBM per device.

v0:
```python
import functools

import jax
import jax.numpy as jnp
from jax import lax
from jax.experimental import pallas as pl
from jax.experimental.pallas import tpu as pltpu
from jax.sharding import PartitionSpec as P

PAYLOADS = (("core", 0, 3), ("cross_y", 3, 1), ("cross_skew", 4, 1), ("cross_own", 5, 1), ("near", 6, 3), ("za", 9, 1), ("zb", 10, 1))


def swap_pairs(size, first, by=1):
    pairs = []
    for i in range(first, size - by, 2 * by):
        for j in range(i, min(i + by, size - by)):
            pairs += [(j, j + by), (j + by, j)]
    return pairs


def place_of(code, group_odd, dev_odd, pair_odd):
    near = code < 5
    up = code < 8
    off = jnp.where(near, code - 2, jnp.where(up, code - 6, code - 9))
    sub = jnp.where(off == 0, 2, jnp.where(off == 1 - 2 * dev_odd, 0, 1))
    to_core = up == (group_odd == 0)
    crossing = jnp.where(to_core, 0, 3) + sub
    far = jnp.where(off == 2 - 4 * pair_odd, 9, 10)
    close = jnp.where(jnp.abs(off) == 2, far, 6 + sub)
    return jnp.where(near, close, crossing)


def places(targets):
    slots = targets.shape[1]
    group = lax.axis_index("group")
    dev = lax.axis_index("dev")
    args = (lax.rem(group, 2), lax.rem(dev, 2), lax.rem(lax.div(dev, 2), 2))
    return [place_of(targets[0, c], *args) for c in range(slots)]


def in_hbm(array):
    return pltpu.with_memory_space_constraint(array, pltpu.HBM)


def fetch(sources, held, sems):
    copies = [pltpu.make_async_copy(source, ref, sems.at[i]) for i, (source, ref) in enumerate(zip(sources, held))]
    for copy in copies:
        copy.start()
    return copies


def slot_kernel(shift, parts, *refs):
    meta, (couplings, history), refs = refs[:3], refs[3:5], refs[5:]
    outs = refs[: len(parts)]
    targets, delays, counts, place, flags, weights, bands, total, zero, in_sems, out_sems, sems = refs[len(parts) :]
    copies = fetch(meta, (targets, delays, counts), sems)
    zero[...] = jnp.zeros_like(zero)
    for copy in copies:
        copy.wait()
    slots = targets.shape[1]
    band = couplings.shape[2]
    low = parts[0][1]
    high = parts[-1][1] + parts[-1][2]
    at = places(targets)
    live = [(c < counts[0]) & (at[c] >= low) & (at[c] < high) for c in range(slots)]

    def band_copies(c):
        lowest = delays[0, c] - 1 - shift
        if shift == 0:
            return [(None, pltpu.make_async_copy(history.at[pl.ds(lowest, band)], bands.at[c], in_sems.at[1, c]))]
        whole = pltpu.make_async_copy(
            history.at[pl.ds(jnp.maximum(lowest, 0), band)], bands.at[c], in_sems.at[1, c]
        )
        later = pltpu.make_async_copy(
            history.at[pl.ds(0, band - 1)], bands.at[c, pl.ds(1, band - 1)], in_sems.at[1, c]
        )
        return [(lowest >= 0, whole), (lowest < 0, later)]

    for c in range(slots):
        @pl.when(live[c])
        def _(c=c):
            pltpu.make_async_copy(couplings.at[0, c], weights.at[c], in_sems.at[0, c]).start()
            for cond, copy in band_copies(c):
                if cond is None:
                    copy.start()
                else:
                    pl.when(cond)(copy.start)
            if shift:
                @pl.when(delays[0, c] - 1 - shift < 0)
                def _():
                    bands[c, 0] = jnp.zeros(bands.shape[2:], bands.dtype)

    for c in range(slots):
        before = functools.reduce(jnp.logical_or, [live[b] & (at[b] == at[c]) for b in range(c)], False)
        after = functools.reduce(jnp.logical_or, [live[b] & (at[b] == at[c]) for b in range(c + 1, slots)], False)
        place[c] = at[c] - low
        flags[0, c] = live[c].astype(jnp.int32)
        flags[1, c] = jnp.int32(before) if isinstance(before, bool) else before.astype(jnp.int32)
        flags[2, c] = jnp.int32(after) if isinstance(after, bool) else after.astype(jnp.int32)

    row_copies = []
    for (_, first, rows), out in zip(parts, outs):
        for r in range(rows):
            p = first + r
            used = functools.reduce(jnp.logical_or, [live[c] & (at[c] == p) for c in range(slots)])
            row_copies.append((p - low, out.at[r], used))
    for p, out, used in row_copies:
        @pl.when(jnp.logical_not(used))
        def _(p=p, out=out):
            pltpu.make_async_copy(zero, out, out_sems.at[p]).start()

    def step(c, carry):
        @pl.when(flags[0, c] != 0)
        def _():
            pltpu.make_async_copy(couplings.at[0, c], weights.at[c], in_sems.at[0, c]).wait()
            if shift == 0:
                pltpu.make_async_copy(history.at[pl.ds(0, band)], bands.at[c], in_sems.at[1, c]).wait()
            else:
                @pl.when(delays[0, c] - 1 - shift >= 0)
                def _():
                    pltpu.make_async_copy(history.at[pl.ds(0, band)], bands.at[c], in_sems.at[1, c]).wait()

                @pl.when(delays[0, c] - 1 - shift < 0)
                def _():
                    pltpu.make_async_copy(
                        history.at[pl.ds(0, band - 1)], bands.at[c, pl.ds(1, band - 1)], in_sems.at[1, c]
                    ).wait()
            lhs = jnp.concatenate([weights[c, w] for w in range(band)], axis=1)
            rhs = bands[c].reshape(band * bands.shape[2], bands.shape[3])
            product = jnp.dot(lhs, rhs, preferred_element_type=jnp.float32)
            p = place[c]

            @pl.when(flags[1, c] == 0)
            def _():
                total[p] = product

            @pl.when(flags[1, c] != 0)
            def _():
                total[p] += product

            for q, out, _ in row_copies:
                @pl.when((p == q) & (flags[2, c] == 0))
                def _(q=q, out=out):
                    pltpu.make_async_copy(total.at[q], out, out_sems.at[q]).start()

        return carry

    lax.fori_loop(0, slots, step, 0)
    for p, out, _ in row_copies:
        pltpu.make_async_copy(zero, out, out_sems.at[p]).wait()


def slot_terms(shift, parts, couplings, history, targets, delays, counts):
    _, slots, band, unknowns, _ = couplings.shape
    width = history.shape[2]
    rows = sum(part[2] for part in parts)
    flops = 2 * slots * band * unknowns * unknowns * width // 2
    return pl.pallas_call(
        functools.partial(slot_kernel, shift, parts),
        out_shape=[jax.ShapeDtypeStruct((part[2], unknowns, width), jnp.float32) for part in parts],
        in_specs=[pl.BlockSpec(memory_space=pl.ANY)] * 5,
        out_specs=[pl.BlockSpec(memory_space=pl.ANY)] * len(parts),
        scratch_shapes=[
            pltpu.SMEM(targets.shape, jnp.int32),
            pltpu.SMEM(delays.shape, jnp.int32),
            pltpu.SMEM(counts.shape, jnp.int32),
            pltpu.SMEM((slots,), jnp.int32),
            pltpu.SMEM((3, slots), jnp.int32),
            pltpu.VMEM((slots, band, unknowns, unknowns), jnp.bfloat16),
            pltpu.VMEM((slots, band, unknowns, width), jnp.bfloat16),
            pltpu.VMEM((rows, unknowns, width), jnp.float32),
            pltpu.VMEM((unknowns, width), jnp.float32),
            pltpu.SemaphoreType.DMA((2, slots)),
            pltpu.SemaphoreType.DMA((rows,)),
            pltpu.SemaphoreType.DMA((3,)),
        ],
        compiler_params=pltpu.CompilerParams(vmem_limit_bytes=40 * 2**20),
        cost_estimate=pl.CostEstimate(flops=flops, bytes_accessed=10 * 2**20, transcendentals=0),
    )(in_hbm(targets), in_hbm(delays), counts, in_hbm(couplings), in_hbm(history))


def field_of(terms):
    near, core_in, *arrived = terms
    return functools.reduce(lambda a, b: a + b, [near[2], core_in[2]] + [term[0] for term in arrived])


def march_kernel(*refs):
    n = len(PAYLOADS)
    meta, (couplings, inverse, incident), terms = refs[:3], refs[3:6], refs[6:13]
    outs = refs[13 + n : 13 + 2 * n]
    current = refs[13 + 2 * n]
    targets, delays, counts, weights, held, in_sems, sem, sems = refs[14 + 2 * n :]
    for copy in fetch(meta, (targets, delays, counts), sems):
        copy.wait()
    slots = targets.shape[1]
    at = places(targets)
    fresh = [(c < counts[0]) & (delays[0, c] == 1) for c in range(slots)]
    for c in range(slots):
        @pl.when(fresh[c])
        def _(c=c):
            pltpu.make_async_copy(couplings.at[0, c, 0], weights.at[c], in_sems.at[c]).start()
    field = field_of(terms)
    right = (incident[0].astype(jnp.float32) - field).astype(jnp.bfloat16)
    current[...] = jnp.dot(inverse[0], right, preferred_element_type=jnp.float32).astype(jnp.bfloat16)
    for c in range(slots):
        @pl.when(fresh[c])
        def _(c=c):
            pltpu.make_async_copy(couplings.at[0, c, 0], weights.at[c], in_sems.at[c]).wait()
            for (_, first, rows), out in zip(PAYLOADS, outs):
                for r in range(rows):
                    @pl.when(at[c] == first + r)
                    def _(out=out, r=r):
                        copy = pltpu.make_async_copy(out.at[r], held, sem)
                        copy.start()
                        copy.wait()
            held[...] += jnp.dot(weights[c], current[...], preferred_element_type=jnp.float32)
            for (_, first, rows), out in zip(PAYLOADS, outs):
                for r in range(rows):
                    @pl.when(at[c] == first + r)
                    def _(out=out, r=r):
                        copy = pltpu.make_async_copy(held, out.at[r], sem)
                        copy.start()
                        copy.wait()


def march(couplings, inverse, incident, targets, delays, counts, sums, payloads):
    _, slots, _, unknowns, _ = couplings.shape
    width = incident.shape[2]
    n = len(payloads)
    vmem = pl.BlockSpec(memory_space=pltpu.VMEM)
    hbm = pl.BlockSpec(memory_space=pl.ANY)
    *updated, current = pl.pallas_call(
        march_kernel,
        out_shape=[jax.ShapeDtypeStruct(p.shape, p.dtype) for p in payloads]
        + [jax.ShapeDtypeStruct((unknowns, width), jnp.bfloat16)],
        in_specs=[pl.BlockSpec(memory_space=pl.ANY)] * 4 + [vmem] * 9 + [hbm] * n,
        out_specs=[hbm] * n + [vmem],
        input_output_aliases={13 + i: i for i in range(n)},
        scratch_shapes=[
            pltpu.SMEM(targets.shape, jnp.int32),
            pltpu.SMEM(delays.shape, jnp.int32),
            pltpu.SMEM(counts.shape, jnp.int32),
            pltpu.VMEM((slots, unknowns, unknowns), jnp.bfloat16),
            pltpu.VMEM((unknowns, width), jnp.float32),
            pltpu.SemaphoreType.DMA((slots,)),
            pltpu.SemaphoreType.DMA,
            pltpu.SemaphoreType.DMA((3,)),
        ],
        compiler_params=pltpu.CompilerParams(vmem_limit_bytes=24 * 2**20),
        cost_estimate=pl.CostEstimate(flops=2 * unknowns * unknowns * width, bytes_accessed=2**21, transcendentals=0),
    )(in_hbm(targets), in_hbm(delays), counts, in_hbm(couplings), inverse, incident, *sums, *payloads)
    return current, updated


def finish_kernel(inverse, incident, *refs):
    *terms, earlier, out = refs
    field = field_of(terms)
    right = (incident[1].astype(jnp.float32) - field).astype(jnp.bfloat16)
    out[0] = earlier[...]
    out[1] = jnp.dot(inverse[0], right, preferred_element_type=jnp.float32).astype(jnp.bfloat16)


def finish(inverse, incident, sums, earlier):
    vmem = pl.BlockSpec(memory_space=pltpu.VMEM)
    return pl.pallas_call(
        finish_kernel,
        out_shape=jax.ShapeDtypeStruct(incident.shape, jnp.bfloat16),
        in_specs=[vmem] * (3 + len(sums)),
        out_specs=vmem,
        compiler_params=pltpu.CompilerParams(vmem_limit_bytes=16 * 2**20),
    )(inverse, incident, *sums, earlier)


def on_chip(kernel, *operands, carried=()):
    vmem = pl.BlockSpec(memory_space=pltpu.VMEM)
    hbm = pl.BlockSpec(memory_space=pl.ANY)
    return pl.pallas_call(
        kernel,
        out_shape=[jax.ShapeDtypeStruct(operands[0].shape, jnp.float32)]
        + [jax.ShapeDtypeStruct(c.shape, c.dtype) for c in carried],
        in_specs=[vmem] * len(operands) + [hbm] * len(carried),
        out_specs=[vmem] + [hbm] * len(carried),
        input_output_aliases={len(operands) + i: 1 + i for i in range(len(carried))},
        compiler_params=pltpu.CompilerParams(vmem_limit_bytes=16 * 2**20),
    )(*operands, *carried)


def join_kernel(row, arrived, near, core_in, *refs):
    total = refs[len(refs) // 2]
    total[0] = arrived[0] + near[row] + core_in[row]


def deliver(groups, devs, payloads):
    core, cross_y, cross_skew, cross_own, near, za, zb = payloads
    x_pairs = swap_pairs(groups, 1)
    skew_in = lax.ppermute(cross_skew, "group", x_pairs)
    y_in = lax.ppermute(cross_y, "group", x_pairs)
    core_in = lax.ppermute(core, "group", swap_pairs(groups, 0))
    za_in = lax.ppermute(za, "dev", swap_pairs(devs, 0, 2))
    zb_in = lax.ppermute(zb, "dev", swap_pairs(devs, 2, 2))
    (skew,) = on_chip(functools.partial(join_kernel, 1), skew_in, near, core_in)
    skew_in = lax.ppermute(skew, "dev", swap_pairs(devs, 1))
    y, cross_own = on_chip(functools.partial(join_kernel, 0), y_in, near, core_in, carried=(cross_own,))
    y_in = lax.ppermute(y, "dev", swap_pairs(devs, 0))
    own_in = lax.ppermute(cross_own, "group", x_pairs)
    return near, core_in, za_in, zb_in, own_in, skew_in, y_in


def shards(groups, devs, couplings, history, inverse, incident, targets, delays, counts):
    meta = (targets, delays, counts)
    first = slot_terms(0, PAYLOADS[:3], couplings, history, *meta)
    second = slot_terms(0, PAYLOADS[3:], couplings, history, *meta)
    later = slot_terms(1, PAYLOADS, couplings, history, *meta)
    sums = deliver(groups, devs, (*first, *second))
    current, payloads = march(couplings, inverse, incident, *meta, sums, later)
    sums = deliver(groups, devs, payloads)
    return finish(inverse, incident, sums, current)


def solution(mesh):
    placed = (
        P(("group", "dev"), None, None, None, None),
        P(None, ("group", "dev"), None),
        P(("group", "dev"), None, None),
        P(None, ("group", "dev"), None),
        P(("group", "dev"), None),
        P(("group", "dev"), None),
        P(("group", "dev")),
    )
    return jax.shard_map(
        functools.partial(shards, mesh.shape["group"], mesh.shape["dev"]),
        mesh=mesh,
        in_specs=placed,
        out_specs=P(None, ("group", "dev"), None),
        check_vma=False,
    )
```

profile of v0, /device:TPU:13, one launch (start us, length us, event | category | flops | bytes accessed | tf_op | source)
XLA Modules:
  0.0 78.9 jit_solution(6443906779544329176)
XLA Ops:
  0.7 4.6 %shard_map.74 = (f32[3,512,256]{2,1,0:T(8,128)S(1)}, f32[1,512,256]{2,1,0:T(8,128)S(1)}, f32[1,512,256]{2,1,0:T(8,128)S(1)}) custom-call(s32[1,6]{1,0:T(1,128)} %refs_0_.7, s32[1,6]{1,0:T(1,128)} %refs_1_.7, s32[1]{0:T(128)S(6)} %copy.26.refs_2_, bf16[1,6,4,512,512]{4,3,2,1,0:T(8,128)(2,1)} %refs_3_.7, bf16[32,512,256]{2,1,0:T(8,128)(2,1)} %refs_4_.6), custom_call_target="tpu_custom_call" | custom-call | flops 1610612736 | bytes 10485760 | tf_op jit(solution)/shard_map/pallas_call | solution.py:158
  5.3 0.1 collective-permute-start
  5.4 4.4 %collective-permute-start.3 = (f32[1,512,256]{2,1,0:T(8,128)S(1)}, f32[1,512,256]{2,1,0:T(8,128)S(1)}, u32[]{:S(2)}, u32[]{:S(2)}) collective-permute-start(f32[1,512,256]{2,1,0:T(8,128)S(1)} %get-tuple-element.35), channel_id=1, source_target_pairs={{8,16},{16,8},{9,17},{17,9},{10,18},{18,10},{11,19},{19,11},{12,20... | collective-permute-start | bytes 1572872 | tf_op jit(solution)/shard_map/ppermute | solution.py:297
  9.7 1.9 %collective-permute-start.5 = (f32[1,512,256]{2,1,0:T(8,128)S(1)}, f32[1,512,256]{2,1,0:T(8,128)S(1)}, u32[]{:S(2)}, u32[]{:S(2)}) collective-permute-start(f32[1,512,256]{2,1,0:T(8,128)S(1)} %get-tuple-element.38), channel_id=1, source_target_pairs={{8,16},{16,8},{9,17},{17,9},{10,18},{18,10},{11,19},{19,11},{12,20... | collective-permute-start | bytes 1572872 | tf_op jit(solution)/shard_map/ppermute | solution.py:296
  11.6 3.7 %shard_map.73 = (f32[1,512,256]{2,1,0:T(8,128)S(1)}, f32[3,512,256]{2,1,0:T(8,128)S(1)}, f32[1,512,256]{2,1,0:T(8,128)S(1)}, f32[1,512,256]{2,1,0:T(8,128)S(1)}) custom-call(s32[1,6]{1,0:T(1,128)} %refs_0_.7, s32[1,6]{1,0:T(1,128)} %refs_1_.7, s32[1]{0:T(128)S(6)} %copy.26.refs_2_, bf16[1,6,4,512,512]{4,3,2,1,0:T(8,128)(2,1)} %refs_3_.7, ...), custom_call_target="tpu_custom_call" | custom-call | flops 1610612736 | bytes 10485760 | tf_op jit(solution)/shard_map/pallas_call | solution.py:158
  15.4 0.3 collective-permute-start.1
  15.6 5.4 %collective-permute-start.2 = (f32[1,512,256]{2,1,0:T(8,128)S(1)}, f32[1,512,256]{2,1,0:T(8,128)S(1)}, u32[]{:S(2)}, u32[]{:S(2)}) collective-permute-start(f32[1,512,256]{2,1,0:T(8,128)S(1)} %get-tuple-element.34), channel_id=1, source_target_pairs={{2,4},{4,2},{3,5},{5,3},{10,12},{12,10},{11,13},{13,11},{18,20},{2... | collective-permute-start | bytes 1572872 | tf_op jit(solution)/shard_map/ppermute | solution.py:300
  21.0 0.0 collective-permute-done.3.arrived
  21.0 0.0 collective-permute-done.core_in.refs_7_
  21.0 0.1 shard_map.75
  21.1 6.0 %collective-permute-start.4 = (f32[1,512,256]{2,1,0:T(8,128)S(1)}, f32[1,512,256]{2,1,0:T(8,128)S(1)}, u32[]{:S(2)}, u32[]{:S(2)}) collective-permute-start(f32[1,512,256]{2,1,0:T(8,128)S(1)} %get-tuple-element.37), channel_id=1, source_target_pairs={{8,16},{16,8},{9,17},{17,9},{10,18},{18,10},{11,19},{19,11},{12,20... | collective-permute-start | bytes 1572872 | tf_op jit(solution)/shard_map/ppermute | solution.py:305
  27.1 0.1 collective-permute-start.7
  27.2 0.0 collective-permute-done.5.arrived
  27.2 0.1 shard_map.76
  27.3 0.0 copy-start
  27.3 0.0 copy-start.1
  27.3 2.9 %collective-permute-start.6 = (f32[1,512,256]{2,1,0:T(8,128)S(1)}, f32[1,512,256]{2,1,0:T(8,128)S(1)}, u32[]{:S(2)}, u32[]{:S(2)}) collective-permute-start(f32[1,512,256]{2,1,0:T(8,128)S(1)} %shard_map.76), channel_id=1, source_target_pairs={{1,2},{2,1},{3,4},{4,3},{5,6},{6,5},{9,10},{10,9},{11,12},{12,11},... | collective-permute-start | bytes 1572872 | tf_op jit(solution)/shard_map/ppermute | solution.py:302
  30.3 5.7 %shard_map.77 = (f32[3,512,256]{2,1,0:T(8,128)S(1)}, f32[1,512,256]{2,1,0:T(8,128)S(1)}, f32[1,512,256]{2,1,0:T(8,128)S(1)}, f32[1,512,256]{2,1,0:T(8,128)S(1)},...) custom-call(s32[1,6]{1,0:T(1,128)} %refs_0_.7, s32[1,6]{1,0:T(1,128)} %refs_1_.7, ...), custom_call_target="tpu_custom_call" | custom-call | flops 1610612736 | bytes 10485760 | tf_op jit(solution)/shard_map/pallas_call | solution.py:158
  36.0 0.0 collective-permute-done.1.refs_8_
  36.0 0.0 collective-permute-done.2.refs_9_
  36.0 0.0 collective-permute-done.4.refs_10_
  36.0 8.0 %collective-permute-done.7.refs_12_ = f32[1,512,256]{2,1,0:T(8,128)S(1)} collective-permute-done((f32[1,512,256]{2,1,0:T(8,128)S(1)}, f32[1,512,256]{2,1,0:T(8,128)S(1)}, u32[]{:S(2)}, u32[]{:S(2)}) %collective-permute-start.7) | collective-permute-done | bytes 524320 | tf_op jit(solution)/shard_map/ppermute | solution.py:304
  44.0 0.0 collective-permute-done.6.refs_11_
  44.0 0.0 copy-done
  44.0 0.0 copy-done.1
  44.0 1.2 %shard_map.78 = (f32[3,512,256]{2,1,0:T(8,128)S(1)}, f32[1,512,256]{2,1,0:T(8,128)S(1)}, f32[1,512,256]{2,1,0:T(8,128)S(1)}, f32[1,512,256]{2,1,0:T(8,128)S(1)},...) custom-call(s32[1,6]{1,0:T(1,128)} %refs_0_.7, ...), custom_call_target="tpu_custom_call", output_to_operand_aliasing={{0}: (13, {}), {1}: (14, {}), {2}: (15, {}), {3}: (16, {}),... | custom-call | flops 134217728 | bytes 2097152 | tf_op jit(solution)/shard_map/pallas_call | solution.py:232
  45.3 0.1 collective-permute-start.8
  45.4 4.7 %collective-permute-start.11 = (f32[1,512,256]{2,1,0:T(8,128)S(1)}, f32[1,512,256]{2,1,0:T(8,128)S(1)}, u32[]{:S(2)}, u32[]{:S(2)}) collective-permute-start(f32[1,512,256]{2,1,0:T(8,128)S(1)} %get-tuple-element.51), channel_id=1, source_target_pairs={{8,16},{16,8},{9,17},{17,9},{10,18},{18,10},{11,19},{19,11},{12,20... | collective-permute-start | bytes 1572872 | tf_op jit(solution)/shard_map/ppermute | solution.py:297
  50.1 1.9 %collective-permute-start.13 = (f32[1,512,256]{2,1,0:T(8,128)S(1)}, f32[1,512,256]{2,1,0:T(8,128)S(1)}, u32[]{:S(2)}, u32[]{:S(2)}) collective-permute-start(f32[1,512,256]{2,1,0:T(8,128)S(1)} %get-tuple-element.54), channel_id=1, source_target_pairs={{8,16},{16,8},{9,17},{17,9},{10,18},{18,10},{11,19},{19,11},{12,20... | collective-permute-start | bytes 1572872 | tf_op jit(solution)/shard_map/ppermute | solution.py:296
  52.0 0.1 collective-permute-start.9
  52.1 1.9 %collective-permute-start.10 = (f32[1,512,256]{2,1,0:T(8,128)S(1)}, f32[1,512,256]{2,1,0:T(8,128)S(1)}, u32[]{:S(2)}, u32[]{:S(2)}) collective-permute-start(f32[1,512,256]{2,1,0:T(8,128)S(1)} %get-tuple-element.50), channel_id=1, source_target_pairs={{2,4},{4,2},{3,5},{5,3},{10,12},{12,10},{11,13},{13,11},{18,20},{2... | collective-permute-start | bytes 1572872 | tf_op jit(solution)/shard_map/ppermute | solution.py:300
  54.0 3.2 %collective-permute-done.11.arrived = f32[1,512,256]{2,1,0:T(8,128)S(1)} collective-permute-done((f32[1,512,256]{2,1,0:T(8,128)S(1)}, f32[1,512,256]{2,1,0:T(8,128)S(1)}, u32[]{:S(2)}, u32[]{:S(2)}) %collective-permute-start.11) | collective-permute-done | bytes 524320 | tf_op jit(solution)/shard_map/ppermute | solution.py:297
  57.2 0.0 collective-permute-done.8.core_in.refs_1_
  57.2 0.1 shard_map.79
  57.3 3.3 %collective-permute-start.12 = (f32[1,512,256]{2,1,0:T(8,128)S(1)}, f32[1,512,256]{2,1,0:T(8,128)S(1)}, u32[]{:S(2)}, u32[]{:S(2)}) collective-permute-start(f32[1,512,256]{2,1,0:T(8,128)S(1)} %get-tuple-element.53), channel_id=1, source_target_pairs={{8,16},{16,8},{9,17},{17,9},{10,18},{18,10},{11,19},{19,11},{12,20... | collective-permute-start | bytes 1572872 | tf_op jit(solution)/shard_map/ppermute | solution.py:305
  60.7 0.1 collective-permute-start.15
  60.8 2.1 %collective-permute-done.13.arrived = f32[1,512,256]{2,1,0:T(8,128)S(1)} collective-permute-done((f32[1,512,256]{2,1,0:T(8,128)S(1)}, f32[1,512,256]{2,1,0:T(8,128)S(1)}, u32[]{:S(2)}, u32[]{:S(2)}) %collective-permute-start.13) | collective-permute-done | bytes 524320 | tf_op jit(solution)/shard_map/ppermute | solution.py:296
  62.9 0.1 shard_map.80
  62.9 2.6 %collective-permute-start.14 = (f32[1,512,256]{2,1,0:T(8,128)S(1)}, f32[1,512,256]{2,1,0:T(8,128)S(1)}, u32[]{:S(2)}, u32[]{:S(2)}) collective-permute-start(f32[1,512,256]{2,1,0:T(8,128)S(1)} %shard_map.80), channel_id=1, source_target_pairs={{1,2},{2,1},{3,4},{4,3},{5,6},{6,5},{9,10},{10,9},{11,12},{12,11},... | collective-permute-start | bytes 1572872 | tf_op jit(solution)/shard_map/ppermute | solution.py:302
  65.6 0.5 collective-permute-done.9.refs_2_
  66.1 0.0 collective-permute-done.10.refs_3_
  66.1 2.4 %collective-permute-done.12.refs_4_ = f32[1,512,256]{2,1,0:T(8,128)S(1)} collective-permute-done((f32[1,512,256]{2,1,0:T(8,128)S(1)}, f32[1,512,256]{2,1,0:T(8,128)S(1)}, u32[]{:S(2)}, u32[]{:S(2)}) %collective-permute-start.12) | collective-permute-done | bytes 524320 | tf_op jit(solution)/shard_map/ppermute | solution.py:305
  68.5 9.2 %collective-permute-done.15.refs_6_ = f32[1,512,256]{2,1,0:T(8,128)S(1)} collective-permute-done((f32[1,512,256]{2,1,0:T(8,128)S(1)}, f32[1,512,256]{2,1,0:T(8,128)S(1)}, u32[]{:S(2)}, u32[]{:S(2)}) %collective-permute-start.15) | collective-permute-done | bytes 524320 | tf_op jit(solution)/shard_map/ppermute | solution.py:304
  77.7 0.0 collective-permute-done.14.refs_5_
  77.7 1.2 %shard_map.81 = bf16[2,512,256]{2,1,0:T(8,128)(2,1)} custom-call(bf16[1,512,512]{2,1,0:T(8,128)(2,1)S(1)} %copy-done, bf16[2,512,256]{2,1,0:T(8,128)(2,1)S(1)} %copy-done.1, f32[3,512,256]{2,1,0:T(8,128)S(1)} %get-tuple-element.47.near.refs_0_, f32[3,512,256]{2,1,0:T(8,128)S(1)} %collective-permute-done.8.core_in.refs_1_, ...), custom_call_target="tpu_custom_call" | custom-call | tf_op jit(solution)/shard_map/pallas_call | solution.py:265
Async XLA Ops:
  5.3 15.8 %collective-permute-start = (f32[3,512,256]{2,1,0:T(8,128)S(1)}, f32[3,512,256]{2,1,0:T(8,128)S(1)}, u32[]{:S(2)}, u32[]{:S(2)}) collective-permute-start(f32[3,512,256]{2,1,0:T(8,128)S(1)} %get-tuple-element.32), channel_id=1, source_target_pairs={{0,8},{8,0},{16,24},{24,16},{1,9},{9,1},{17,25},{25,17},{2,10},{10... | collective-permute-start | bytes 4718600 | tf_op jit(solution)/shard_map/ppermute | solution.py:298
  5.4 15.7 %collective-permute-start.3 = (f32[1,512,256]{2,1,0:T(8,128)S(1)}, f32[1,512,256]{2,1,0:T(8,128)S(1)}, u32[]{:S(2)}, u32[]{:S(2)}) collective-permute-start(f32[1,512,256]{2,1,0:T(8,128)S(1)} %get-tuple-element.35), channel_id=1, source_target_pairs={{8,16},{16,8},{9,17},{17,9},{10,18},{18,10},{11,19},{19,11},{12,20... | collective-permute-start | bytes 1572872 | tf_op jit(solution)/shard_map/ppermute | solution.py:297
  9.7 17.5 %collective-permute-start.5 = (f32[1,512,256]{2,1,0:T(8,128)S(1)}, f32[1,512,256]{2,1,0:T(8,128)S(1)}, u32[]{:S(2)}, u32[]{:S(2)}) collective-permute-start(f32[1,512,256]{2,1,0:T(8,128)S(1)} %get-tuple-element.38), channel_id=1, source_target_pairs={{8,16},{16,8},{9,17},{17,9},{10,18},{18,10},{11,19},{19,11},{12,20... | collective-permute-start | bytes 1572872 | tf_op jit(solution)/shard_map/ppermute | solution.py:296
  15.4 20.6 %collective-permute-start.1 = (f32[1,512,256]{2,1,0:T(8,128)S(1)}, f32[1,512,256]{2,1,0:T(8,128)S(1)}, u32[]{:S(2)}, u32[]{:S(2)}) collective-permute-start(f32[1,512,256]{2,1,0:T(8,128)S(1)} %get-tuple-element.33), channel_id=1, source_target_pairs={{0,2},{2,0},{1,3},{3,1},{4,6},{6,4},{5,7},{7,5},{8,10},{10,8},{9,1... | collective-permute-start | bytes 1572872 | tf_op jit(solution)/shard_map/ppermute | solution.py:299
  15.6 20.4 %collective-permute-start.2 = (f32[1,512,256]{2,1,0:T(8,128)S(1)}, f32[1,512,256]{2,1,0:T(8,128)S(1)}, u32[]{:S(2)}, u32[]{:S(2)}) collective-permute-start(f32[1,512,256]{2,1,0:T(8,128)S(1)} %get-tuple-element.34), channel_id=1, source_target_pairs={{2,4},{4,2},{3,5},{5,3},{10,12},{12,10},{11,13},{13,11},{18,20},{2... | collective-permute-start | bytes 1572872 | tf_op jit(solution)/shard_map/ppermute | solution.py:300
  21.1 14.9 %collective-permute-start.4 = (f32[1,512,256]{2,1,0:T(8,128)S(1)}, f32[1,512,256]{2,1,0:T(8,128)S(1)}, u32[]{:S(2)}, u32[]{:S(2)}) collective-permute-start(f32[1,512,256]{2,1,0:T(8,128)S(1)} %get-tuple-element.37), channel_id=1, source_target_pairs={{8,16},{16,8},{9,17},{17,9},{10,18},{18,10},{11,19},{19,11},{12,20... | collective-permute-start | bytes 1572872 | tf_op jit(solution)/shard_map/ppermute | solution.py:305
  27.1 16.9 %collective-permute-start.7 = (f32[1,512,256]{2,1,0:T(8,128)S(1)}, f32[1,512,256]{2,1,0:T(8,128)S(1)}, u32[]{:S(2)}, u32[]{:S(2)}) collective-permute-start(f32[1,512,256]{2,1,0:T(8,128)S(1)} %get-tuple-element.39), channel_id=1, source_target_pairs={{0,1},{1,0},{2,3},{3,2},{4,5},{5,4},{6,7},{7,6},{8,9},{9,8},{10,11... | collective-permute-start | bytes 1572872 | tf_op jit(solution)/shard_map/ppermute | solution.py:304
  27.3 16.7 %copy-start = (bf16[1,512,512]{2,1,0:T(8,128)(2,1)S(1)}, bf16[1,512,512]{2,1,0:T(8,128)(2,1)}, u32[]{:S(2)}) copy-start(bf16[1,512,512]{2,1,0:T(8,128)(2,1)} %inverse.1) | copy-start | bytes 1572868
  27.3 16.7 %copy-start.1 = (bf16[2,512,256]{2,1,0:T(8,128)(2,1)S(1)}, bf16[2,512,256]{2,1,0:T(8,128)(2,1)}, u32[]{:S(2)}) copy-start(bf16[2,512,256]{2,1,0:T(8,128)(2,1)} %incident.1) | copy-start | bytes 1572868
  27.3 16.7 %collective-permute-start.6 = (f32[1,512,256]{2,1,0:T(8,128)S(1)}, f32[1,512,256]{2,1,0:T(8,128)S(1)}, u32[]{:S(2)}, u32[]{:S(2)}) collective-permute-start(f32[1,512,256]{2,1,0:T(8,128)S(1)} %shard_map.76), channel_id=1, source_target_pairs={{1,2},{2,1},{3,4},{4,3},{5,6},{6,5},{9,10},{10,9},{11,12},{12,11},... | collective-permute-start | bytes 1572872 | tf_op jit(solution)/shard_map/ppermute | solution.py:302
  45.3 12.0 %collective-permute-start.8 = (f32[3,512,256]{2,1,0:T(8,128)S(1)}, f32[3,512,256]{2,1,0:T(8,128)S(1)}, u32[]{:S(2)}, u32[]{:S(2)}) collective-permute-start(f32[3,512,256]{2,1,0:T(8,128)S(1)} %get-tuple-element.48), channel_id=1, source_target_pairs={{0,8},{8,0},{16,24},{24,16},{1,9},{9,1},{17,25},{25,17},{2,10},{10... | collective-permute-start | bytes 4718600 | tf_op jit(solution)/shard_map/ppermute | solution.py:298
  45.4 11.9 %collective-permute-start.11 = (f32[1,512,256]{2,1,0:T(8,128)S(1)}, f32[1,512,256]{2,1,0:T(8,128)S(1)}, u32[]{:S(2)}, u32[]{:S(2)}) collective-permute-start(f32[1,512,256]{2,1,0:T(8,128)S(1)} %get-tuple-element.51), channel_id=1, source_target_pairs={{8,16},{16,8},{9,17},{17,9},{10,18},{18,10},{11,19},{19,11},{12,20... | collective-permute-start | bytes 1572872 | tf_op jit(solution)/shard_map/ppermute | solution.py:297
  50.1 12.8 %collective-permute-start.13 = (f32[1,512,256]{2,1,0:T(8,128)S(1)}, f32[1,512,256]{2,1,0:T(8,128)S(1)}, u32[]{:S(2)}, u32[]{:S(2)}) collective-permute-start(f32[1,512,256]{2,1,0:T(8,128)S(1)} %get-tuple-element.54), channel_id=1, source_target_pairs={{8,16},{16,8},{9,17},{17,9},{10,18},{18,10},{11,19},{19,11},{12,20... | collective-permute-start | bytes 1572872 | tf_op jit(solution)/shard_map/ppermute | solution.py:296
  52.0 14.1 %collective-permute-start.9 = (f32[1,512,256]{2,1,0:T(8,128)S(1)}, f32[1,512,256]{2,1,0:T(8,128)S(1)}, u32[]{:S(2)}, u32[]{:S(2)}) collective-permute-start(f32[1,512,256]{2,1,0:T(8,128)S(1)} %get-tuple-element.49), channel_id=1, source_target_pairs={{0,2},{2,0},{1,3},{3,1},{4,6},{6,4},{5,7},{7,5},{8,10},{10,8},{9,1... | collective-permute-start | bytes 1572872 | tf_op jit(solution)/shard_map/ppermute | solution.py:299
  52.1 14.0 %collective-permute-start.10 = (f32[1,512,256]{2,1,0:T(8,128)S(1)}, f32[1,512,256]{2,1,0:T(8,128)S(1)}, u32[]{:S(2)}, u32[]{:S(2)}) collective-permute-start(f32[1,512,256]{2,1,0:T(8,128)S(1)} %get-tuple-element.50), channel_id=1, source_target_pairs={{2,4},{4,2},{3,5},{5,3},{10,12},{12,10},{11,13},{13,11},{18,20},{2... | collective-permute-start | bytes 1572872 | tf_op jit(solution)/shard_map/ppermute | solution.py:300
  57.3 11.1 %collective-permute-start.12 = (f32[1,512,256]{2,1,0:T(8,128)S(1)}, f32[1,512,256]{2,1,0:T(8,128)S(1)}, u32[]{:S(2)}, u32[]{:S(2)}) collective-permute-start(f32[1,512,256]{2,1,0:T(8,128)S(1)} %get-tuple-element.53), channel_id=1, source_target_pairs={{8,16},{16,8},{9,17},{17,9},{10,18},{18,10},{11,19},{19,11},{12,20... | collective-permute-start | bytes 1572872 | tf_op jit(solution)/shard_map/ppermute | solution.py:305
  60.7 17.0 %collective-permute-start.15 = (f32[1,512,256]{2,1,0:T(8,128)S(1)}, f32[1,512,256]{2,1,0:T(8,128)S(1)}, u32[]{:S(2)}, u32[]{:S(2)}) collective-permute-start(f32[1,512,256]{2,1,0:T(8,128)S(1)} %get-tuple-element.55), channel_id=1, source_target_pairs={{0,1},{1,0},{2,3},{3,2},{4,5},{5,4},{6,7},{7,6},{8,9},{9,8},{10,11... | collective-permute-start | bytes 1572872 | tf_op jit(solution)/shard_map/ppermute | solution.py:304
  62.9 14.7 %collective-permute-start.14 = (f32[1,512,256]{2,1,0:T(8,128)S(1)}, f32[1,512,256]{2,1,0:T(8,128)S(1)}, u32[]{:S(2)}, u32[]{:S(2)}) collective-permute-start(f32[1,512,256]{2,1,0:T(8,128)S(1)} %shard_map.80), channel_id=1, source_target_pairs={{1,2},{2,1},{3,4},{4,3},{5,6},{6,5},{9,10},{10,9},{11,12},{12,11},... | collective-permute-start | bytes 1572872 | tf_op jit(solution)/shard_map/ppermute | solution.py:302
where the time goes:
time: 78.8 us; the launch traced here: 78.9 us
  starting transfers between devices  35.8 us (45%)
  waiting for transfers between devices  25.4 us (32%)
  Pallas kernels  16.8 us (21%)
  between operations  0.9 us (1%)
    ppermute x2, waiting for transfers between devices, deliver(): y_in = lax.ppermute(y, 'dev', swap_pairs(devs, 0))  17.2 us
    pallas_call x3, Pallas kernels, slot_terms(): pl.pallas_call(functools.partial(slot_kernel, shift, parts), out_shape=[j...  14 us
    ppermute x2, starting transfers between devices, deliver(): own_in = lax.ppermute(cross_own, 'group', x_pairs)  9.36 us
    ppermute x2, starting transfers between devices, deliver(): y_in = lax.ppermute(cross_y, 'group', x_pairs)  9.09 us
    ppermute x2, starting transfers between devices, deliver(): zb_in = lax.ppermute(zb, 'dev', swap_pairs(devs, 2, 2))  7.3 us
    ppermute x2, starting transfers between devices, deliver(): skew_in = lax.ppermute(skew, 'dev', swap_pairs(devs, 1))  5.56 us
    ppermute x2, starting transfers between devices, deliver(): skew_in = lax.ppermute(cross_skew, 'group', x_pairs)  3.84 us
    ppermute x2, waiting for transfers between devices, deliver(): y_in = lax.ppermute(cross_y, 'group', x_pairs)  3.21 us
  transfers between devices with their start and end apart: 16, of which 6 were waited for; matrix products, arithmetic and copies ran while one was open for 0% of the time, Pallas kernels for 12%

commit v1 on v0

v1 whole, which is shorter than its diff:
```python
import functools

import jax
import jax.numpy as jnp
from jax import lax
from jax.experimental import pallas as pl
from jax.experimental.pallas import tpu as pltpu
from jax.sharding import PartitionSpec as P

CORE, NEAR, CROSS, ZA, ZB = 0, 3, 6, 9, 10
PAYLOADS = (
    ("core", CORE, 3),
    ("near", NEAR, 3),
    ("cross_y", CROSS, 1),
    ("cross_skew", CROSS + 1, 1),
    ("cross_own", CROSS + 2, 1),
    ("za", ZA, 1),
    ("zb", ZB, 1),
)


def swap_pairs(size, first, by=1):
    pairs = []
    for i in range(first, size - by, 2 * by):
        for j in range(i, min(i + by, size - by)):
            pairs += [(j, j + by), (j + by, j)]
    return pairs


def far_pairs(groups, devs, turn):
    return [
        (g * devs + a, g * devs + b)
        for g in range(groups)
        for a, b in swap_pairs(devs, 2 * ((g + turn) % 2), 2)
    ]


def places(targets):
    group, dev = lax.axis_index("group"), lax.axis_index("dev")
    group_odd, dev_odd, pair_odd = lax.rem(group, 2), lax.rem(dev, 2), lax.rem(lax.div(dev, 2), 2)
    at, useful = [], []
    for c in range(targets.shape[1]):
        code = targets[0, c]
        near = code < 5
        up = code < 8
        off = jnp.where(near, code - 2, jnp.where(up, code - 6, code - 9))
        sub = jnp.where(off == 0, 2, jnp.where(off == 1 - 2 * dev_odd, 0, 1))
        to_core = up == (group_odd == 0)
        crossing = jnp.where(to_core, CORE + sub, CROSS + sub)
        far = jnp.where(off == 2 - 4 * lax.rem(pair_odd + group_odd, 2), ZA, ZB)
        close = jnp.where(jnp.abs(off) == 2, far, NEAR + sub)
        at.append(jnp.where(near, close, crossing))
        to_group = group + jnp.where(near, 0, jnp.where(up, 1, -1))
        to_dev = dev + off
        inside = (to_group >= 0) & (to_group < lax.axis_size("group"))
        useful.append(inside & (to_dev >= 0) & (to_dev < lax.axis_size("dev")))
    return at, useful


def in_hbm(array):
    return pltpu.with_memory_space_constraint(array, pltpu.HBM)


def fetch(sources, held, sems):
    copies = [pltpu.make_async_copy(source, ref, sems.at[i]) for i, (source, ref) in enumerate(zip(sources, held))]
    for copy in copies:
        copy.start()
    return copies


def rows_of(parts, outs):
    return [(first + r, out, r) for (_, first, rows), out in zip(parts, outs) for r in range(rows)]


def slot_kernel(shift, parts, unread, *refs):
    meta, (couplings, history), refs = refs[:3], refs[3:5], refs[5 + unread :]
    outs = refs[: len(parts)]
    targets, delays, counts, place, flags, weights, bands, total, in_sems, sems = refs[len(parts) :]
    for copy in fetch(meta, (targets, delays, counts), sems):
        copy.wait()
    slots = targets.shape[1]
    band = couplings.shape[2]
    rows = rows_of(parts, outs)
    at, useful = places(targets)
    live = []
    for c in range(slots):
        wanted = (at[c] >= rows[0][0]) & (at[c] <= rows[-1][0])
        live.append((c < counts[0]) & useful[c] & wanted)

    def copies_of(c, early):
        matrices = pltpu.make_async_copy(couplings.at[0, c], weights.at[c], in_sems.at[0, c])
        if early:
            source = history.at[pl.ds(0, band - 1)]
            steps = pltpu.make_async_copy(source, bands.at[c, pl.ds(1, band - 1)], in_sems.at[1, c])
        else:
            source = history.at[pl.ds(jnp.maximum(delays[0, c] - 1 - shift, 0), band)]
            steps = pltpu.make_async_copy(source, bands.at[c], in_sems.at[1, c])
        return matrices, steps

    def each(c, act):
        if shift == 0:
            act(copies_of(c, False))
            return
        early = delays[0, c] <= shift

        @pl.when(early)
        def _():
            act(copies_of(c, True))

        @pl.when(jnp.logical_not(early))
        def _():
            act(copies_of(c, False))

    def start(copies):
        for copy in copies:
            copy.start()

    def wait(copies):
        for copy in copies:
            copy.wait()

    for c in range(slots):
        @pl.when(live[c])
        def _(c=c):
            each(c, start)
            if shift:
                @pl.when(delays[0, c] <= shift)
                def _():
                    bands[c, 0] = jnp.zeros(bands.shape[2:], bands.dtype)

    for c in range(slots):
        place[c] = at[c]
        flags[0, c] = live[c].astype(jnp.int32)
        repeats = [(live[b] & (at[b] == at[c])).astype(jnp.int32) for b in range(c)]
        flags[1, c] = functools.reduce(lambda x, y: x | y, repeats, jnp.int32(0))

    for p, out, r in rows:
        used = functools.reduce(jnp.logical_or, [live[c] & (at[c] == p) for c in range(slots)])

        @pl.when(jnp.logical_not(used))
        def _(out=out, r=r):
            out[r] = jnp.zeros(out.shape[1:], out.dtype)

    def step(c, carry):
        @pl.when(flags[0, c] != 0)
        def _():
            each(c, wait)
            lhs = jnp.concatenate([weights[c, w] for w in range(band)], axis=1)
            rhs = bands[c].reshape(band * bands.shape[2], bands.shape[3])
            total[...] = jnp.dot(lhs, rhs, preferred_element_type=jnp.float32)
            for p, out, r in rows:
                @pl.when((place[c] == p) & (flags[1, c] == 0))
                def _(out=out, r=r):
                    out[r] = total[...]

                @pl.when((place[c] == p) & (flags[1, c] != 0))
                def _(out=out, r=r):
                    out[r] += total[...]

        return carry

    lax.fori_loop(0, slots, step, 0)


def slot_terms(shift, parts, couplings, history, targets, delays, counts, earlier=()):
    _, slots, band, unknowns, _ = couplings.shape
    width = history.shape[2]
    flops = slots * band * unknowns * unknowns * width
    return pl.pallas_call(
        functools.partial(slot_kernel, shift, parts, len(earlier)),
        out_shape=[jax.ShapeDtypeStruct((part[2], unknowns, width), jnp.float32) for part in parts],
        in_specs=[pl.BlockSpec(memory_space=pl.ANY)] * (5 + len(earlier)),
        out_specs=[pl.BlockSpec(memory_space=pltpu.VMEM)] * len(parts),
        scratch_shapes=[
            pltpu.SMEM(targets.shape, jnp.int32),
            pltpu.SMEM(delays.shape, jnp.int32),
            pltpu.SMEM(counts.shape, jnp.int32),
            pltpu.SMEM((slots,), jnp.int32),
            pltpu.SMEM((2, slots), jnp.int32),
            pltpu.VMEM((slots, band, unknowns, unknowns), jnp.bfloat16),
            pltpu.VMEM((slots, band, unknowns, width), jnp.bfloat16),
            pltpu.VMEM((unknowns, width), jnp.float32),
            pltpu.SemaphoreType.DMA((2, slots)),
            pltpu.SemaphoreType.DMA((3,)),
        ],
        compiler_params=pltpu.CompilerParams(vmem_limit_bytes=30 * 2**20),
        cost_estimate=pl.CostEstimate(flops=flops, bytes_accessed=10 * 2**20, transcendentals=0),
    )(in_hbm(targets), in_hbm(delays), counts, in_hbm(couplings), in_hbm(history), *earlier)


def march_kernel(*refs):
    n = len(PAYLOADS)
    meta, (couplings, inverse, incident), terms = refs[:3], refs[3:6], refs[6:8]
    outs = refs[8 + n : 8 + 2 * n]
    current = refs[8 + 2 * n]
    targets, delays, counts, weights, held, in_sems, sem, sems = refs[9 + 2 * n :]
    for copy in fetch(meta, (targets, delays, counts), sems):
        copy.wait()
    slots = targets.shape[1]
    at, useful = places(targets)
    fresh = [(c < counts[0]) & (delays[0, c] == 1) & useful[c] for c in range(slots)]
    for c in range(slots):
        @pl.when(fresh[c])
        def _(c=c):
            pltpu.make_async_copy(couplings.at[0, c, 0], weights.at[c], in_sems.at[c]).start()
    field = terms[0][0] + terms[1][0]
    right = (incident[0].astype(jnp.float32) - field).astype(jnp.bfloat16)
    current[...] = jnp.dot(inverse[0], right, preferred_element_type=jnp.float32).astype(jnp.bfloat16)
    for c in range(slots):
        @pl.when(fresh[c])
        def _(c=c):
            pltpu.make_async_copy(couplings.at[0, c, 0], weights.at[c], in_sems.at[c]).wait()
            for p, out, r in rows_of(PAYLOADS, outs):
                @pl.when(at[c] == p)
                def _(out=out, r=r):
                    copy = pltpu.make_async_copy(out.at[r], held, sem)
                    copy.start()
                    copy.wait()
            held[...] += jnp.dot(weights[c], current[...], preferred_element_type=jnp.float32)
            for p, out, r in rows_of(PAYLOADS, outs):
                @pl.when(at[c] == p)
                def _(out=out, r=r):
                    copy = pltpu.make_async_copy(held, out.at[r], sem)
                    copy.start()
                    copy.wait()


def march(couplings, inverse, incident, targets, delays, counts, sums, payloads):
    _, slots, _, unknowns, _ = couplings.shape
    width = incident.shape[2]
    n = len(payloads)
    vmem = pl.BlockSpec(memory_space=pltpu.VMEM)
    hbm = pl.BlockSpec(memory_space=pl.ANY)
    *updated, current = pl.pallas_call(
        march_kernel,
        out_shape=[jax.ShapeDtypeStruct(p.shape, p.dtype) for p in payloads]
        + [jax.ShapeDtypeStruct((unknowns, width), jnp.bfloat16)],
        in_specs=[pl.BlockSpec(memory_space=pl.ANY)] * 4 + [vmem] * 4 + [hbm] * n,
        out_specs=[hbm] * n + [vmem],
        input_output_aliases={8 + i: i for i in range(n)},
        scratch_shapes=[
            pltpu.SMEM(targets.shape, jnp.int32),
            pltpu.SMEM(delays.shape, jnp.int32),
            pltpu.SMEM(counts.shape, jnp.int32),
            pltpu.VMEM((slots, unknowns, unknowns), jnp.bfloat16),
            pltpu.VMEM((unknowns, width), jnp.float32),
            pltpu.SemaphoreType.DMA((slots,)),
            pltpu.SemaphoreType.DMA,
            pltpu.SemaphoreType.DMA((3,)),
        ],
        compiler_params=pltpu.CompilerParams(vmem_limit_bytes=24 * 2**20),
        cost_estimate=pl.CostEstimate(flops=2 * unknowns * unknowns * width, bytes_accessed=2**21, transcendentals=0),
    )(in_hbm(targets), in_hbm(delays), counts, in_hbm(couplings), inverse, incident, *sums, *payloads)
    return current, updated


def finish_kernel(inverse, incident, *refs):
    *terms, earlier, out = refs
    field = terms[0][0] + terms[1][0]
    right = (incident[1].astype(jnp.float32) - field).astype(jnp.bfloat16)
    out[0] = earlier[...]
    out[1] = jnp.dot(inverse[0], right, preferred_element_type=jnp.float32).astype(jnp.bfloat16)


def finish(inverse, incident, sums, earlier):
    vmem = pl.BlockSpec(memory_space=pltpu.VMEM)
    return pl.pallas_call(
        finish_kernel,
        out_shape=jax.ShapeDtypeStruct(incident.shape, jnp.bfloat16),
        in_specs=[vmem] * (3 + len(sums)),
        out_specs=vmem,
        compiler_params=pltpu.CompilerParams(vmem_limit_bytes=16 * 2**20),
    )(inverse, incident, *sums, earlier)


def stage(kernel, operands, carried=()):
    vmem = pl.BlockSpec(memory_space=pltpu.VMEM)
    hbm = pl.BlockSpec(memory_space=pl.ANY)
    sums = [jax.ShapeDtypeStruct(operands[0].shape, jnp.float32)]
    return pl.pallas_call(
        kernel,
        out_shape=sums + [jax.ShapeDtypeStruct(c.shape, c.dtype) for c in carried],
        in_specs=[vmem] * len(operands) + [hbm] * len(carried),
        out_specs=[vmem] * len(sums) + [hbm] * len(carried),
        input_output_aliases={len(operands) + i: len(sums) + i for i in range(len(carried))},
        compiler_params=pltpu.CompilerParams(vmem_limit_bytes=16 * 2**20),
    )(*operands, *carried)


def join_kernel(row, arrived, near, core_in, *refs):
    total = refs[len(refs) // 2]
    total[0] = arrived[0] + near[row] + core_in[row]


def sum_kernel(*refs):
    *terms, total = refs
    total[...] = functools.reduce(lambda a, b: a + b, [term[...] for term in terms])


def deliver(groups, devs, payloads):
    core, near, cross_y, cross_skew, cross_own, za, zb = payloads
    x_pairs = swap_pairs(groups, 1)
    y_in = lax.ppermute(cross_y, "group", x_pairs)
    skew_in = lax.ppermute(cross_skew, "group", x_pairs)
    core_in = lax.ppermute(core, "group", swap_pairs(groups, 0))
    za_in = lax.ppermute(za, ("group", "dev"), far_pairs(groups, devs, 0))
    y, zb = stage(functools.partial(join_kernel, 0), (y_in, near, core_in), (zb,))
    y_in = lax.ppermute(y, "dev", swap_pairs(devs, 0))
    zb_in = lax.ppermute(zb, ("group", "dev"), far_pairs(groups, devs, 1))
    skew, own = stage(functools.partial(join_kernel, 1), (skew_in, near, core_in), (cross_own,))
    skew_in = lax.ppermute(skew, "dev", swap_pairs(devs, 1))
    own_in = lax.ppermute(own, "group", x_pairs)
    (field,) = stage(functools.partial(join_kernel, 2), (za_in, near, core_in))
    (field,) = stage(sum_kernel, (field, y_in))
    (field,) = stage(sum_kernel, (field, zb_in))
    (field,) = stage(sum_kernel, (field, skew_in))
    return field, own_in


def shards(groups, devs, couplings, history, inverse, incident, targets, delays, counts):
    meta = (targets, delays, counts)
    first = slot_terms(0, PAYLOADS[:4], couplings, history, *meta)
    second = slot_terms(0, PAYLOADS[4:], couplings, history, *meta, first[:1])
    later = slot_terms(1, PAYLOADS, couplings, history, *meta)
    sums = deliver(groups, devs, (*first, *second))
    current, payloads = march(couplings, inverse, incident, *meta, sums, later)
    sums = deliver(groups, devs, payloads)
    return finish(inverse, incident, sums, current)


def solution(mesh):
    placed = (
        P(("group", "dev"), None, None, None, None),
        P(None, ("group", "dev"), None),
        P(("group", "dev"), None, None),
        P(None, ("group", "dev"), None),
        P(("group", "dev"), None),
        P(("group", "dev"), None),
        P(("group", "dev")),
    )
    return jax.shard_map(
        functools.partial(shards, mesh.shape["group"], mesh.shape["dev"]),
        mesh=mesh,
        in_specs=placed,
        out_specs=P(None, ("group", "dev"), None),
        check_vma=False,
    )
```

time: 78.8 us -> 79.5 us (level); the launches traced: 78.9 us -> 78.8 us
  Pallas kernels: 16.8 us -> 13.6 us
  starting transfers between devices: 35.8 us -> 38.9 us
    ppermute x2, waiting for transfers between devices: 17.2 us -> 6.39 us  [deliver(): y_in = lax.ppermute(y, 'dev', swap_pairs(devs, 0))]
    ppermute x2, waiting for transfers between devices: 0.01 us -> 9.01 us  [deliver(): skew_in = lax.ppermute(skew, 'dev', swap_pairs(devs, 1))]
    ppermute x2, starting transfers between devices: 9.09 us -> 3.82 us  [deliver(): y_in = lax.ppermute(cross_y, 'group', x_pairs)]
    ppermute x2, starting transfers between devices: 3.84 us -> 7.28 us  [deliver(): skew_in = lax.ppermute(cross_skew, 'group', x_pairs)]
    ppermute x2, starting transfers between devices: 0.14 us -> 3.38 us  [deliver(): core_in = lax.ppermute(core, 'group', swap_pairs(groups, 0))]
    pallas_call x7 -> x15, Pallas kernels: 14.3 us -> 11.3 us  [the longest x3 10.5 us: slot_terms(): pl.pallas_call(functools.partial(slot_kernel, shift, parts, len(earlier))...]
    ppermute x2, waiting for transfers between devices: 2.1 us -> 4.53 us  [deliver(): skew_in = lax.ppermute(cross_skew, 'group', x_pairs)]
    ppermute x2, starting transfers between devices: 0.14 us -> 1.58 us  [deliver(): y_in = lax.ppermute(y, 'dev', swap_pairs(devs, 0))]
  transfers between devices with their start and end apart: 16 -> 16, of which waited for: 6 -> 7; matrix products, arithmetic and copies ran while one was open for 0% -> 0% of each run, Pallas kernels for 12% -> 9%
where the time goes in v1:
time: 79.5 us; the launch traced here: 78.8 us
  starting transfers between devices  38.9 us (49%)
  waiting for transfers between devices  25.4 us (32%)
  Pallas kernels  13.6 us (17%)
  between operations  0.95 us (1%)
    pallas_call x3, Pallas kernels, slot_terms(): pl.pallas_call(functools.partial(slot_kernel, shift, parts, len(earlier))...  10.5 us
    ppermute x2, waiting for transfers between devices, deliver(): skew_in = lax.ppermute(skew, 'dev', swap_pairs(devs, 1))  9.01 us
    ppermute x2, starting transfers between devices, deliver(): skew_in = lax.ppermute(cross_skew, 'group', x_pairs)  7.28 us
    ppermute x2, starting transfers between devices, deliver(): za_in = lax.ppermute(za, ('group', 'dev'), far_pairs(groups, devs, 0))  6.97 us
    ppermute x2, starting transfers between devices, deliver(): skew_in = lax.ppermute(skew, 'dev', swap_pairs(devs, 1))  6.66 us
    ppermute x2, waiting for transfers between devices, deliver(): y_in = lax.ppermute(y, 'dev', swap_pairs(devs, 0))  6.39 us
    ppermute x2, starting transfers between devices, deliver(): own_in = lax.ppermute(own, 'group', x_pairs)  5.32 us
    ppermute x2, waiting for transfers between devices, deliver(): skew_in = lax.ppermute(cross_skew, 'group', x_pairs)  4.53 us
  transfers between devices with their start and end apart: 16, of which 7 were waited for; matrix products, arithmetic and copies ran while one was open for 0% of the time, Pallas kernels for 9%

profile of v1, /device:TPU:13, one launch (start us, length us, event | category | flops | bytes accessed | tf_op | source)
XLA Modules:
  0.0 78.8 jit_solution(8987569162191507353)
XLA Ops:
  0.7 4.6 %shard_map.73 = (f32[3,512,256]{2,1,0:T(8,128)S(1)}, f32[3,512,256]{2,1,0:T(8,128)S(1)}, f32[1,512,256]{2,1,0:T(8,128)S(1)}, f32[1,512,256]{2,1,0:T(8,128)S(1)}) custom-call(s32[1,6]{1,0:T(1,128)} %refs_0_.7, s32[1,6]{1,0:T(1,128)} %refs_1_.7, s32[1]{0:T(128)S(6)} %copy.30.refs_2_, bf16[1,6,4,512,512]{4,3,2,1,0:T(8,128)(2,1)} %refs_3_.7, ...), custom_call_target="tpu_custom_call" | custom-call | flops 1610612736 | bytes 10485760 | tf_op jit(solution)/shard_map/pallas_call | solution.py:169
  5.2 1.6 %collective-permute-start.1 = (f32[3,512,256]{2,1,0:T(8,128)S(1)}, f32[3,512,256]{2,1,0:T(8,128)S(1)}, u32[]{:S(2)}, u32[]{:S(2)}) collective-permute-start(f32[3,512,256]{2,1,0:T(8,128)S(1)} %get-tuple-element.35.refs_5_), channel_id=1, source_target_pairs={{0,8},{8,0},{16,24},{24,16},{1,9},{9,1},{17,25},{25,17},{2,10},{10... | collective-permute-start | bytes 4718600 | tf_op jit(solution)/shard_map/ppermute | solution.py:305
  6.9 1.9 %collective-permute-start.2 = (f32[1,512,256]{2,1,0:T(8,128)S(1)}, f32[1,512,256]{2,1,0:T(8,128)S(1)}, u32[]{:S(2)}, u32[]{:S(2)}) collective-permute-start(f32[1,512,256]{2,1,0:T(8,128)S(1)} %get-tuple-element.38), channel_id=1, source_target_pairs={{8,16},{16,8},{9,17},{17,9},{10,18},{18,10},{11,19},{19,11},{12,20... | collective-permute-start | bytes 1572872 | tf_op jit(solution)/shard_map/ppermute | solution.py:303
  8.8 3.6 %collective-permute-start.5 = (f32[1,512,256]{2,1,0:T(8,128)S(1)}, f32[1,512,256]{2,1,0:T(8,128)S(1)}, u32[]{:S(2)}, u32[]{:S(2)}) collective-permute-start(f32[1,512,256]{2,1,0:T(8,128)S(1)} %get-tuple-element.42), channel_id=1, source_target_pairs={{8,16},{16,8},{9,17},{17,9},{10,18},{18,10},{11,19},{19,11},{12,20... | collective-permute-start | bytes 1572872 | tf_op jit(solution)/shard_map/ppermute | solution.py:304
  12.4 1.2 %shard_map.74 = (f32[1,512,256]{2,1,0:T(8,128)S(1)}, f32[1,512,256]{2,1,0:T(8,128)S(1)}, f32[1,512,256]{2,1,0:T(8,128)S(1)}) custom-call(s32[1,6]{1,0:T(1,128)} %refs_0_.7, s32[1,6]{1,0:T(1,128)} %refs_1_.7, s32[1]{0:T(128)S(6)} %copy.30.refs_2_, bf16[1,6,4,512,512]{4,3,2,1,0:T(8,128)(2,1)} %refs_3_.7, bf16[32,512,256]{2,1,0:T(8,128)(2,1)} %refs_4_.6, ...), custom_call_target="tpu_custom_call" | custom-call | flops 1610612736 | bytes 10485760 | tf_op jit(solution)/shard_map/pallas_call | solution.py:169
  13.7 5.1 %collective-permute-start = (f32[1,512,256]{2,1,0:T(8,128)S(1)}, f32[1,512,256]{2,1,0:T(8,128)S(1)}, u32[]{:S(2)}, u32[]{:S(2)}) collective-permute-start(f32[1,512,256]{2,1,0:T(8,128)S(1)} %get-tuple-element.36), channel_id=1, source_target_pairs={{0,2},{2,0},{1,3},{3,1},{4,6},{6,4},{5,7},{7,5},{10,12},{12,10},{1... | collective-permute-start | bytes 1572872 | tf_op jit(solution)/shard_map/ppermute | solution.py:306
  18.7 0.0 collective-permute-done.2.arrived
  18.7 0.0 collective-permute-done.1.core_in
  18.7 0.1 shard_map.76
  18.8 1.4 %collective-permute-start.3 = (f32[1,512,256]{2,1,0:T(8,128)S(1)}, f32[1,512,256]{2,1,0:T(8,128)S(1)}, u32[]{:S(2)}, u32[]{:S(2)}) collective-permute-start(f32[1,512,256]{2,1,0:T(8,128)S(1)} %get-tuple-element.40), channel_id=1, source_target_pairs={{0,1},{1,0},{2,3},{3,2},{4,5},{5,4},{6,7},{7,6},{8,9},{9,8},{10,11... | collective-permute-start | bytes 1572872 | tf_op jit(solution)/shard_map/ppermute | solution.py:308
  20.2 1.9 %collective-permute-start.4 = (f32[1,512,256]{2,1,0:T(8,128)S(1)}, f32[1,512,256]{2,1,0:T(8,128)S(1)}, u32[]{:S(2)}, u32[]{:S(2)}) collective-permute-start(f32[1,512,256]{2,1,0:T(8,128)S(1)} %get-tuple-element.41), channel_id=1, source_target_pairs={{2,4},{4,2},{3,5},{5,3},{8,10},{10,8},{9,11},{11,9},{12,14},{14,12... | collective-permute-start | bytes 1572872 | tf_op jit(solution)/shard_map/ppermute | solution.py:309
  22.1 1.1 %collective-permute-done.5.arrived = f32[1,512,256]{2,1,0:T(8,128)S(1)} collective-permute-done((f32[1,512,256]{2,1,0:T(8,128)S(1)}, f32[1,512,256]{2,1,0:T(8,128)S(1)}, u32[]{:S(2)}, u32[]{:S(2)}) %collective-permute-start.5) | collective-permute-done | bytes 524320 | tf_op jit(solution)/shard_map/ppermute | solution.py:304
  23.3 0.1 shard_map.79
  23.4 2.3 %collective-permute-start.6 = (f32[1,512,256]{2,1,0:T(8,128)S(1)}, f32[1,512,256]{2,1,0:T(8,128)S(1)}, u32[]{:S(2)}, u32[]{:S(2)}) collective-permute-start(f32[1,512,256]{2,1,0:T(8,128)S(1)} %get-tuple-element.44), channel_id=1, source_target_pairs={{1,2},{2,1},{3,4},{4,3},{5,6},{6,5},{9,10},{10,9},{11,12},{12,11},... | collective-permute-start | bytes 1572872 | tf_op jit(solution)/shard_map/ppermute | solution.py:311
  25.6 3.4 %collective-permute-start.7 = (f32[1,512,256]{2,1,0:T(8,128)S(1)}, f32[1,512,256]{2,1,0:T(8,128)S(1)}, u32[]{:S(2)}, u32[]{:S(2)}) collective-permute-start(f32[1,512,256]{2,1,0:T(8,128)S(1)} %get-tuple-element.45), channel_id=1, source_target_pairs={{8,16},{16,8},{9,17},{17,9},{10,18},{18,10},{11,19},{19,11},{12,20... | collective-permute-start | bytes 1572872 | tf_op jit(solution)/shard_map/ppermute | solution.py:312
  29.1 4.7 %shard_map.81 = (f32[3,512,256]{2,1,0:T(8,128)S(1)}, f32[3,512,256]{2,1,0:T(8,128)S(1)}, f32[1,512,256]{2,1,0:T(8,128)S(1)}, f32[1,512,256]{2,1,0:T(8,128)S(1)},...) custom-call(s32[1,6]{1,0:T(1,128)} %refs_0_.7, s32[1,6]{1,0:T(1,128)} %refs_1_.7, ...), custom_call_target="tpu_custom_call" | custom-call | flops 1610612736 | bytes 10485760 | tf_op jit(solution)/shard_map/pallas_call | solution.py:169
  33.8 0.0 collective-permute-done.arrived
  33.8 0.1 shard_map.75.refs_0_
  33.9 6.4 %collective-permute-done.3.refs_1_ = f32[1,512,256]{2,1,0:T(8,128)S(1)} collective-permute-done((f32[1,512,256]{2,1,0:T(8,128)S(1)}, f32[1,512,256]{2,1,0:T(8,128)S(1)}, u32[]{:S(2)}, u32[]{:S(2)}) %collective-permute-start.3) | collective-permute-done | bytes 524320 | tf_op jit(solution)/shard_map/ppermute | solution.py:308
  40.3 0.1 shard_map.77.refs_0_
  40.3 0.0 copy-start
  40.4 0.0 copy-start.1
  40.4 0.0 collective-permute-done.4.refs_1_
  40.4 0.1 shard_map.78.refs_0_
  40.4 1.1 %collective-permute-done.6.refs_1_ = f32[1,512,256]{2,1,0:T(8,128)S(1)} collective-permute-done((f32[1,512,256]{2,1,0:T(8,128)S(1)}, f32[1,512,256]{2,1,0:T(8,128)S(1)}, u32[]{:S(2)}, u32[]{:S(2)}) %collective-permute-start.6) | collective-permute-done | bytes 524320 | tf_op jit(solution)/shard_map/ppermute | solution.py:311
  41.6 0.1 shard_map.80.refs_6_
  41.6 0.0 collective-permute-done.7.refs_7_
  41.6 0.0 copy-done
  41.7 0.0 copy-done.1
  41.7 1.1 %shard_map.82 = (f32[3,512,256]{2,1,0:T(8,128)S(1)}, f32[3,512,256]{2,1,0:T(8,128)S(1)}, f32[1,512,256]{2,1,0:T(8,128)S(1)}, f32[1,512,256]{2,1,0:T(8,128)S(1)},...) custom-call(s32[1,6]{1,0:T(1,128)} %refs_0_.7, ...), custom_call_target="tpu_custom_call", output_to_operand_aliasing={{0}: (8, {}), {1}: (9, {}), {2}: (10, {}), {3}: (11, {}), {... | custom-call | flops 134217728 | bytes 2097152 | tf_op jit(solution)/shard_map/pallas_call | solution.py:234
  42.8 1.7 %collective-permute-start.9 = (f32[3,512,256]{2,1,0:T(8,128)S(1)}, f32[3,512,256]{2,1,0:T(8,128)S(1)}, u32[]{:S(2)}, u32[]{:S(2)}) collective-permute-start(f32[3,512,256]{2,1,0:T(8,128)S(1)} %get-tuple-element.55), channel_id=1, source_target_pairs={{0,8},{8,0},{16,24},{24,16},{1,9},{9,1},{17,25},{25,17},{2,10},{10... | collective-permute-start | bytes 4718600 | tf_op jit(solution)/shard_map/ppermute | solution.py:305
  44.6 1.9 %collective-permute-start.10 = (f32[1,512,256]{2,1,0:T(8,128)S(1)}, f32[1,512,256]{2,1,0:T(8,128)S(1)}, u32[]{:S(2)}, u32[]{:S(2)}) collective-permute-start(f32[1,512,256]{2,1,0:T(8,128)S(1)} %get-tuple-element.56), channel_id=1, source_target_pairs={{8,16},{16,8},{9,17},{17,9},{10,18},{18,10},{11,19},{19,11},{12,20... | collective-permute-start | bytes 1572872 | tf_op jit(solution)/shard_map/ppermute | solution.py:303
  46.5 3.6 %collective-permute-start.13 = (f32[1,512,256]{2,1,0:T(8,128)S(1)}, f32[1,512,256]{2,1,0:T(8,128)S(1)}, u32[]{:S(2)}, u32[]{:S(2)}) collective-permute-start(f32[1,512,256]{2,1,0:T(8,128)S(1)} %get-tuple-element.60), channel_id=1, source_target_pairs={{8,16},{16,8},{9,17},{17,9},{10,18},{18,10},{11,19},{19,11},{12,20... | collective-permute-start | bytes 1572872 | tf_op jit(solution)/shard_map/ppermute | solution.py:304
  50.1 1.9 %collective-permute-start.8 = (f32[1,512,256]{2,1,0:T(8,128)S(1)}, f32[1,512,256]{2,1,0:T(8,128)S(1)}, u32[]{:S(2)}, u32[]{:S(2)}) collective-permute-start(f32[1,512,256]{2,1,0:T(8,128)S(1)} %get-tuple-element.53), channel_id=1, source_target_pairs={{0,2},{2,0},{1,3},{3,1},{4,6},{6,4},{5,7},{7,5},{10,12},{12,10},{1... | collective-permute-start | bytes 1572872 | tf_op jit(solution)/shard_map/ppermute | solution.py:306
  52.0 3.3 %collective-permute-done.10.arrived = f32[1,512,256]{2,1,0:T(8,128)S(1)} collective-permute-done((f32[1,512,256]{2,1,0:T(8,128)S(1)}, f32[1,512,256]{2,1,0:T(8,128)S(1)}, u32[]{:S(2)}, u32[]{:S(2)}) %collective-permute-start.10) | collective-permute-done | bytes 524320 | tf_op jit(solution)/shard_map/ppermute | solution.py:303
  55.3 0.0 collective-permute-done.9.core_in
  55.3 0.1 shard_map.84
  55.4 0.2 collective-permute-start.11
  55.6 2.0 %collective-permute-start.12 = (f32[1,512,256]{2,1,0:T(8,128)S(1)}, f32[1,512,256]{2,1,0:T(8,128)S(1)}, u32[]{:S(2)}, u32[]{:S(2)}) collective-permute-start(f32[1,512,256]{2,1,0:T(8,128)S(1)} %get-tuple-element.59), channel_id=1, source_target_pairs={{2,4},{4,2},{3,5},{5,3},{8,10},{10,8},{9,11},{11,9},{12,14},{14,12... | collective-permute-start | bytes 1572872 | tf_op jit(solution)/shard_map/ppermute | solution.py:309
  57.6 3.4 %collective-permute-done.13.arrived = f32[1,512,256]{2,1,0:T(8,128)S(1)} collective-permute-done((f32[1,512,256]{2,1,0:T(8,128)S(1)}, f32[1,512,256]{2,1,0:T(8,128)S(1)}, u32[]{:S(2)}, u32[]{:S(2)}) %collective-permute-start.13) | collective-permute-done | bytes 524320 | tf_op jit(solution)/shard_map/ppermute | solution.py:304
  61.0 0.1 shard_map.87
  61.0 4.4 %collective-permute-start.14 = (f32[1,512,256]{2,1,0:T(8,128)S(1)}, f32[1,512,256]{2,1,0:T(8,128)S(1)}, u32[]{:S(2)}, u32[]{:S(2)}) collective-permute-start(f32[1,512,256]{2,1,0:T(8,128)S(1)} %get-tuple-element.62), channel_id=1, source_target_pairs={{1,2},{2,1},{3,4},{4,3},{5,6},{6,5},{9,10},{10,9},{11,12},{12,11},... | collective-permute-start | bytes 1572872 | tf_op jit(solution)/shard_map/ppermute | solution.py:311
  65.4 1.9 %collective-permute-start.15 = (f32[1,512,256]{2,1,0:T(8,128)S(1)}, f32[1,512,256]{2,1,0:T(8,128)S(1)}, u32[]{:S(2)}, u32[]{:S(2)}) collective-permute-start(f32[1,512,256]{2,1,0:T(8,128)S(1)} %get-tuple-element.63), channel_id=1, source_target_pairs={{8,16},{16,8},{9,17},{17,9},{10,18},{18,10},{11,19},{19,11},{12,20... | collective-permute-start | bytes 1572872 | tf_op jit(solution)/shard_map/ppermute | solution.py:312
  67.4 0.0 collective-permute-done.8.arrived
  67.4 0.1 shard_map.83.refs_0_
  67.5 0.0 collective-permute-done.11.refs_1_
  67.5 0.1 shard_map.85.refs_0_
  67.5 2.1 %collective-permute-done.12.refs_1_ = f32[1,512,256]{2,1,0:T(8,128)S(1)} collective-permute-done((f32[1,512,256]{2,1,0:T(8,128)S(1)}, f32[1,512,256]{2,1,0:T(8,128)S(1)}, u32[]{:S(2)}, u32[]{:S(2)}) %collective-permute-start.12) | collective-permute-done | bytes 524320 | tf_op jit(solution)/shard_map/ppermute | solution.py:309
  69.7 0.1 shard_map.86.refs_0_
  69.7 7.9 %collective-permute-done.14.refs_1_ = f32[1,512,256]{2,1,0:T(8,128)S(1)} collective-permute-done((f32[1,512,256]{2,1,0:T(8,128)S(1)}, f32[1,512,256]{2,1,0:T(8,128)S(1)}, u32[]{:S(2)}, u32[]{:S(2)}) %collective-permute-start.14) | collective-permute-done | bytes 524320 | tf_op jit(solution)/shard_map/ppermute | solution.py:311
  77.6 0.1 shard_map.88.refs_0_
  77.7 0.0 collective-permute-done.15.refs_1_
  77.7 1.1 %shard_map.89 = bf16[2,512,256]{2,1,0:T(8,128)(2,1)} custom-call(bf16[1,512,512]{2,1,0:T(8,128)(2,1)S(1)} %copy-done, bf16[2,512,256]{2,1,0:T(8,128)(2,1)S(1)} %copy-done.1, f32[1,512,256]{2,1,0:T(8,128)S(1)} %shard_map.88.refs_0_, f32[1,512,256]{2,1,0:T(8,128)S(1)} %collective-permute-done.15.refs_1_, bf16[512,256]{1,0:T(8,128)(2,1)S(1)} %get-tuple-element.64.refs_2_), custom_call_target="tpu_custom_call" | custom-call | tf_op jit(solution)/shard_map/pallas_call | solution.py:267
Async XLA Ops:
  5.2 13.5 %collective-permute-start.1 = (f32[3,512,256]{2,1,0:T(8,128)S(1)}, f32[3,512,256]{2,1,0:T(8,128)S(1)}, u32[]{:S(2)}, u32[]{:S(2)}) collective-permute-start(f32[3,512,256]{2,1,0:T(8,128)S(1)} %get-tuple-element.35.refs_5_), channel_id=1, source_target_pairs={{0,8},{8,0},{16,24},{24,16},{1,9},{9,1},{17,25},{25,17},{2,10},{10... | collective-permute-start | bytes 4718600 | tf_op jit(solution)/shard_map/ppermute | solution.py:305
  6.9 11.8 %collective-permute-start.2 = (f32[1,512,256]{2,1,0:T(8,128)S(1)}, f32[1,512,256]{2,1,0:T(8,128)S(1)}, u32[]{:S(2)}, u32[]{:S(2)}) collective-permute-start(f32[1,512,256]{2,1,0:T(8,128)S(1)} %get-tuple-element.38), channel_id=1, source_target_pairs={{8,16},{16,8},{9,17},{17,9},{10,18},{18,10},{11,19},{19,11},{12,20... | collective-permute-start | bytes 1572872 | tf_op jit(solution)/shard_map/ppermute | solution.py:303
  8.8 14.5 %collective-permute-start.5 = (f32[1,512,256]{2,1,0:T(8,128)S(1)}, f32[1,512,256]{2,1,0:T(8,128)S(1)}, u32[]{:S(2)}, u32[]{:S(2)}) collective-permute-start(f32[1,512,256]{2,1,0:T(8,128)S(1)} %get-tuple-element.42), channel_id=1, source_target_pairs={{8,16},{16,8},{9,17},{17,9},{10,18},{18,10},{11,19},{19,11},{12,20... | collective-permute-start | bytes 1572872 | tf_op jit(solution)/shard_map/ppermute | solution.py:304
  13.7 20.1 %collective-permute-start = (f32[1,512,256]{2,1,0:T(8,128)S(1)}, f32[1,512,256]{2,1,0:T(8,128)S(1)}, u32[]{:S(2)}, u32[]{:S(2)}) collective-permute-start(f32[1,512,256]{2,1,0:T(8,128)S(1)} %get-tuple-element.36), channel_id=1, source_target_pairs={{0,2},{2,0},{1,3},{3,1},{4,6},{6,4},{5,7},{7,5},{10,12},{12,10},{1... | collective-permute-start | bytes 1572872 | tf_op jit(solution)/shard_map/ppermute | solution.py:306
  18.8 21.4 %collective-permute-start.3 = (f32[1,512,256]{2,1,0:T(8,128)S(1)}, f32[1,512,256]{2,1,0:T(8,128)S(1)}, u32[]{:S(2)}, u32[]{:S(2)}) collective-permute-start(f32[1,512,256]{2,1,0:T(8,128)S(1)} %get-tuple-element.40), channel_id=1, source_target_pairs={{0,1},{1,0},{2,3},{3,2},{4,5},{5,4},{6,7},{7,6},{8,9},{9,8},{10,11... | collective-permute-start | bytes 1572872 | tf_op jit(solution)/shard_map/ppermute | solution.py:308
  20.2 20.1 %collective-permute-start.4 = (f32[1,512,256]{2,1,0:T(8,128)S(1)}, f32[1,512,256]{2,1,0:T(8,128)S(1)}, u32[]{:S(2)}, u32[]{:S(2)}) collective-permute-start(f32[1,512,256]{2,1,0:T(8,128)S(1)} %get-tuple-element.41), channel_id=1, source_target_pairs={{2,4},{4,2},{3,5},{5,3},{8,10},{10,8},{9,11},{11,9},{12,14},{14,12... | collective-permute-start | bytes 1572872 | tf_op jit(solution)/shard_map/ppermute | solution.py:309
  23.4 18.2 %collective-permute-start.6 = (f32[1,512,256]{2,1,0:T(8,128)S(1)}, f32[1,512,256]{2,1,0:T(8,128)S(1)}, u32[]{:S(2)}, u32[]{:S(2)}) collective-permute-start(f32[1,512,256]{2,1,0:T(8,128)S(1)} %get-tuple-element.44), channel_id=1, source_target_pairs={{1,2},{2,1},{3,4},{4,3},{5,6},{6,5},{9,10},{10,9},{11,12},{12,11},... | collective-permute-start | bytes 1572872 | tf_op jit(solution)/shard_map/ppermute | solution.py:311
  25.6 16.0 %collective-permute-start.7 = (f32[1,512,256]{2,1,0:T(8,128)S(1)}, f32[1,512,256]{2,1,0:T(8,128)S(1)}, u32[]{:S(2)}, u32[]{:S(2)}) collective-permute-start(f32[1,512,256]{2,1,0:T(8,128)S(1)} %get-tuple-element.45), channel_id=1, source_target_pairs={{8,16},{16,8},{9,17},{17,9},{10,18},{18,10},{11,19},{19,11},{12,20... | collective-permute-start | bytes 1572872 | tf_op jit(solution)/shard_map/ppermute | solution.py:312
  40.3 1.3 %copy-start = (bf16[1,512,512]{2,1,0:T(8,128)(2,1)S(1)}, bf16[1,512,512]{2,1,0:T(8,128)(2,1)}, u32[]{:S(2)}) copy-start(bf16[1,512,512]{2,1,0:T(8,128)(2,1)} %inverse.1) | copy-start | bytes 1572868
  40.4 1.3 %copy-start.1 = (bf16[2,512,256]{2,1,0:T(8,128)(2,1)S(1)}, bf16[2,512,256]{2,1,0:T(8,128)(2,1)}, u32[]{:S(2)}) copy-start(bf16[2,512,256]{2,1,0:T(8,128)(2,1)} %incident.1) | copy-start | bytes 1572868
  42.8 12.5 %collective-permute-start.9 = (f32[3,512,256]{2,1,0:T(8,128)S(1)}, f32[3,512,256]{2,1,0:T(8,128)S(1)}, u32[]{:S(2)}, u32[]{:S(2)}) collective-permute-start(f32[3,512,256]{2,1,0:T(8,128)S(1)} %get-tuple-element.55), channel_id=1, source_target_pairs={{0,8},{8,0},{16,24},{24,16},{1,9},{9,1},{17,25},{25,17},{2,10},{10... | collective-permute-start | bytes 4718600 | tf_op jit(solution)/shard_map/ppermute | solution.py:305
  44.6 10.8 %collective-permute-start.10 = (f32[1,512,256]{2,1,0:T(8,128)S(1)}, f32[1,512,256]{2,1,0:T(8,128)S(1)}, u32[]{:S(2)}, u32[]{:S(2)}) collective-permute-start(f32[1,512,256]{2,1,0:T(8,128)S(1)} %get-tuple-element.56), channel_id=1, source_target_pairs={{8,16},{16,8},{9,17},{17,9},{10,18},{18,10},{11,19},{19,11},{12,20... | collective-permute-start | bytes 1572872 | tf_op jit(solution)/shard_map/ppermute | solution.py:303
  46.5 14.5 %collective-permute-start.13 = (f32[1,512,256]{2,1,0:T(8,128)S(1)}, f32[1,512,256]{2,1,0:T(8,128)S(1)}, u32[]{:S(2)}, u32[]{:S(2)}) collective-permute-start(f32[1,512,256]{2,1,0:T(8,128)S(1)} %get-tuple-element.60), channel_id=1, source_target_pairs={{8,16},{16,8},{9,17},{17,9},{10,18},{18,10},{11,19},{19,11},{12,20... | collective-permute-start | bytes 1572872 | tf_op jit(solution)/shard_map/ppermute | solution.py:304
  50.1 17.2 %collective-permute-start.8 = (f32[1,512,256]{2,1,0:T(8,128)S(1)}, f32[1,512,256]{2,1,0:T(8,128)S(1)}, u32[]{:S(2)}, u32[]{:S(2)}) collective-permute-start(f32[1,512,256]{2,1,0:T(8,128)S(1)} %get-tuple-element.53), channel_id=1, source_target_pairs={{0,2},{2,0},{1,3},{3,1},{4,6},{6,4},{5,7},{7,5},{10,12},{12,10},{1... | collective-permute-start | bytes 1572872 | tf_op jit(solution)/shard_map/ppermute | solution.py:306
  55.4 12.0 %collective-permute-start.11 = (f32[1,512,256]{2,1,0:T(8,128)S(1)}, f32[1,512,256]{2,1,0:T(8,128)S(1)}, u32[]{:S(2)}, u32[]{:S(2)}) collective-permute-start(f32[1,512,256]{2,1,0:T(8,128)S(1)} %get-tuple-element.58), channel_id=1, source_target_pairs={{0,1},{1,0},{2,3},{3,2},{4,5},{5,4},{6,7},{7,6},{8,9},{9,8},{10,11... | collective-permute-start | bytes 1572872 | tf_op jit(solution)/shard_map/ppermute | solution.py:308
  55.6 14.1 %collective-permute-start.12 = (f32[1,512,256]{2,1,0:T(8,128)S(1)}, f32[1,512,256]{2,1,0:T(8,128)S(1)}, u32[]{:S(2)}, u32[]{:S(2)}) collective-permute-start(f32[1,512,256]{2,1,0:T(8,128)S(1)} %get-tuple-element.59), channel_id=1, source_target_pairs={{2,4},{4,2},{3,5},{5,3},{8,10},{10,8},{9,11},{11,9},{12,14},{14,12... | collective-permute-start | bytes 1572872 | tf_op jit(solution)/shard_map/ppermute | solution.py:309
  61.0 16.6 %collective-permute-start.14 = (f32[1,512,256]{2,1,0:T(8,128)S(1)}, f32[1,512,256]{2,1,0:T(8,128)S(1)}, u32[]{:S(2)}, u32[]{:S(2)}) collective-permute-start(f32[1,512,256]{2,1,0:T(8,128)S(1)} %get-tuple-element.62), channel_id=1, source_target_pairs={{1,2},{2,1},{3,4},{4,3},{5,6},{6,5},{9,10},{10,9},{11,12},{12,11},... | collective-permute-start | bytes 1572872 | tf_op jit(solution)/shard_map/ppermute | solution.py:311
  65.4 12.2 %collective-permute-start.15 = (f32[1,512,256]{2,1,0:T(8,128)S(1)}, f32[1,512,256]{2,1,0:T(8,128)S(1)}, u32[]{:S(2)}, u32[]{:S(2)}) collective-permute-start(f32[1,512,256]{2,1,0:T(8,128)S(1)} %get-tuple-element.63), channel_id=1, source_target_pairs={{8,16},{16,8},{9,17},{17,9},{10,18},{18,10},{11,19},{19,11},{12,20... | collective-permute-start | bytes 1572872 | tf_op jit(solution)/shard_map/ppermute | solution.py:312

commit v2 on v1

--- a/solution.py
+++ b/solution.py
@@ -31,7 +31,7 @@
     return [
         (g * devs + a, g * devs + b)
         for g in range(groups)
-        for a, b in swap_pairs(devs, 2 * ((g + turn) % 2), 2)
+        for a, b in swap_pairs(devs, 2 - 2 * turn, 2)
     ]
 
 
@@ -47,7 +47,7 @@
         sub = jnp.where(off == 0, 2, jnp.where(off == 1 - 2 * dev_odd, 0, 1))
         to_core = up == (group_odd == 0)
         crossing = jnp.where(to_core, CORE + sub, CROSS + sub)
-        far = jnp.where(off == 2 - 4 * lax.rem(pair_odd + group_odd, 2), ZA, ZB)
+        far = jnp.where(off == 2 - 4 * pair_odd, ZB, ZA)
         close = jnp.where(jnp.abs(off) == 2, far, NEAR + sub)
         at.append(jnp.where(near, close, crossing))
         to_group = group + jnp.where(near, 0, jnp.where(up, 1, -1))
@@ -75,12 +75,15 @@
 def slot_kernel(shift, parts, unread, *refs):
     meta, (couplings, history), refs = refs[:3], refs[3:5], refs[5 + unread :]
     outs = refs[: len(parts)]
-    targets, delays, counts, place, flags, weights, bands, total, in_sems, sems = refs[len(parts) :]
-    for copy in fetch(meta, (targets, delays, counts), sems):
+    targets, delays, counts, place, weights, bands, total, in_sems, sems = refs[len(parts) :]
+    copies = fetch(meta, (targets, delays, counts), sems)
+    rows = rows_of(parts, outs)
+    for _, out, r in rows:
+        out[r] = jnp.zeros(out.shape[1:], out.dtype)
+    for copy in copies:
         copy.wait()
     slots = targets.shape[1]
     band = couplings.shape[2]
-    rows = rows_of(parts, outs)
     at, useful = places(targets)
     live = []
     for c in range(slots):
@@ -129,31 +132,17 @@
                     bands[c, 0] = jnp.zeros(bands.shape[2:], bands.dtype)
 
     for c in range(slots):
-        place[c] = at[c]
-        flags[0, c] = live[c].astype(jnp.int32)
-        repeats = [(live[b] & (at[b] == at[c])).astype(jnp.int32) for b in range(c)]
-        flags[1, c] = functools.reduce(lambda x, y: x | y, repeats, jnp.int32(0))
-
-    for p, out, r in rows:
-        used = functools.reduce(jnp.logical_or, [live[c] & (at[c] == p) for c in range(slots)])
-
-        @pl.when(jnp.logical_not(used))
-        def _(out=out, r=r):
-            out[r] = jnp.zeros(out.shape[1:], out.dtype)
+        place[c] = jnp.where(live[c], at[c], -1)
 
     def step(c, carry):
-        @pl.when(flags[0, c] != 0)
+        @pl.when(place[c] >= 0)
         def _():
             each(c, wait)
             lhs = jnp.concatenate([weights[c, w] for w in range(band)], axis=1)
             rhs = bands[c].reshape(band * bands.shape[2], bands.shape[3])
             total[...] = jnp.dot(lhs, rhs, preferred_element_type=jnp.float32)
             for p, out, r in rows:
-                @pl.when((place[c] == p) & (flags[1, c] == 0))
-                def _(out=out, r=r):
-                    out[r] = total[...]
-
-                @pl.when((place[c] == p) & (flags[1, c] != 0))
+                @pl.when(place[c] == p)
                 def _(out=out, r=r):
                     out[r] += total[...]
 
@@ -176,7 +165,6 @@
             pltpu.SMEM(delays.shape, jnp.int32),
             pltpu.SMEM(counts.shape, jnp.int32),
             pltpu.SMEM((slots,), jnp.int32),
-            pltpu.SMEM((2, slots), jnp.int32),
             pltpu.VMEM((slots, band, unknowns, unknowns), jnp.bfloat16),
             pltpu.VMEM((slots, band, unknowns, width), jnp.bfloat16),
             pltpu.VMEM((unknowns, width), jnp.float32),
@@ -307,9 +295,9 @@
     y, zb = stage(functools.partial(join_kernel, 0), (y_in, near, core_in), (zb,))
     y_in = lax.ppermute(y, "dev", swap_pairs(devs, 0))
     zb_in = lax.ppermute(zb, ("group", "dev"), far_pairs(groups, devs, 1))
-    skew, own = stage(functools.partial(join_kernel, 1), (skew_in, near, core_in), (cross_own,))
+    skew, cross_own = stage(functools.partial(join_kernel, 1), (skew_in, near, core_in), (cross_own,))
     skew_in = lax.ppermute(skew, "dev", swap_pairs(devs, 1))
-    own_in = lax.ppermute(own, "group", x_pairs)
+    own_in = lax.ppermute(cross_own, "group", x_pairs)
     (field,) = stage(functools.partial(join_kernel, 2), (za_in, near, core_in))
     (field,) = stage(sum_kernel, (field, y_in))
     (field,) = stage(sum_kernel, (field, zb_in))

time: 79.5 us -> 77.3 us (0.972)
  the two profiles are of different devices: /device:TPU:13 before, /device:TPU:9 now
where the time goes in v2:
time: 77.3 us; the launch traced here: 77.6 us
  starting transfers between devices  34.3 us (44%)
  waiting for transfers between devices  27.2 us (35%)
  Pallas kernels  15.2 us (20%)
  between operations  0.95 us (1%)
    pallas_call x3, Pallas kernels, slot_terms(): pl.pallas_call(functools.partial(slot_kernel, shift, parts, len(earlier))...  12.1 us
    ppermute x2, waiting for transfers between devices, deliver(): skew_in = lax.ppermute(skew, 'dev', swap_pairs(devs, 1))  9.28 us
    ppermute x2, waiting for transfers between devices, deliver(): y_in = lax.ppermute(y, 'dev', swap_pairs(devs, 0))  8.98 us
    ppermute x2, starting transfers between devices, deliver(): za_in = lax.ppermute(za, ('group', 'dev'), far_pairs(groups, devs, 0))  7.72 us
    ppermute x2, waiting for transfers between devices, deliver(): skew_in = lax.ppermute(cross_skew, 'group', x_pairs)  6.85 us
    ppermute x2, starting transfers between devices, deliver(): skew_in = lax.ppermute(cross_skew, 'group', x_pairs)  6.13 us
    ppermute x2, starting transfers between devices, deliver(): y_in = lax.ppermute(cross_y, 'group', x_pairs)  4.98 us
    ppermute x2, starting transfers between devices, deliver(): own_in = lax.ppermute(cross_own, 'group', x_pairs)  4.81 us
  transfers between devices with their start and end apart: 16, of which 8 were waited for; matrix products, arithmetic and copies ran while one was open for 0% of the time, Pallas kernels for 12%

profile of v2, /device:TPU:9, one launch (start us, length us, event | category | flops | bytes accessed | tf_op | source)
XLA Modules:
  0.0 77.6 jit_solution(7438608093952441104)
XLA Ops:
  0.7 3.7 %shard_map.73 = (f32[3,512,256]{2,1,0:T(8,128)S(1)}, f32[3,512,256]{2,1,0:T(8,128)S(1)}, f32[1,512,256]{2,1,0:T(8,128)S(1)}, f32[1,512,256]{2,1,0:T(8,128)S(1)}) custom-call(s32[1,6]{1,0:T(1,128)} %refs_0_.7, s32[1,6]{1,0:T(1,128)} %refs_1_.7, s32[1]{0:T(128)S(6)} %copy.30.refs_2_, bf16[1,6,4,512,512]{4,3,2,1,0:T(8,128)(2,1)} %refs_3_.7, ...), custom_call_target="tpu_custom_call" | custom-call | flops 1610612736 | bytes 10485760 | tf_op jit(solution)/shard_map/pallas_call | solution.py:158
  4.4 4.3 %collective-permute-start.1 = (f32[3,512,256]{2,1,0:T(8,128)S(1)}, f32[3,512,256]{2,1,0:T(8,128)S(1)}, u32[]{:S(2)}, u32[]{:S(2)}) collective-permute-start(f32[3,512,256]{2,1,0:T(8,128)S(1)} %get-tuple-element.35.refs_5_), channel_id=1, source_target_pairs={{0,8},{8,0},{16,24},{24,16},{1,9},{9,1},{17,25},{25,17},{2,10},{10... | collective-permute-start | bytes 4718600 | tf_op jit(solution)/shard_map/ppermute | solution.py:293
  8.7 1.9 %collective-permute-start.2 = (f32[1,512,256]{2,1,0:T(8,128)S(1)}, f32[1,512,256]{2,1,0:T(8,128)S(1)}, u32[]{:S(2)}, u32[]{:S(2)}) collective-permute-start(f32[1,512,256]{2,1,0:T(8,128)S(1)} %get-tuple-element.38), channel_id=1, source_target_pairs={{8,16},{16,8},{9,17},{17,9},{10,18},{18,10},{11,19},{19,11},{12,20... | collective-permute-start | bytes 1572872 | tf_op jit(solution)/shard_map/ppermute | solution.py:291
  10.6 3.6 %collective-permute-start.5 = (f32[1,512,256]{2,1,0:T(8,128)S(1)}, f32[1,512,256]{2,1,0:T(8,128)S(1)}, u32[]{:S(2)}, u32[]{:S(2)}) collective-permute-start(f32[1,512,256]{2,1,0:T(8,128)S(1)} %get-tuple-element.42), channel_id=1, source_target_pairs={{8,16},{16,8},{9,17},{17,9},{10,18},{18,10},{11,19},{19,11},{12,20... | collective-permute-start | bytes 1572872 | tf_op jit(solution)/shard_map/ppermute | solution.py:292
  14.3 3.5 %shard_map.74 = (f32[1,512,256]{2,1,0:T(8,128)S(1)}, f32[1,512,256]{2,1,0:T(8,128)S(1)}, f32[1,512,256]{2,1,0:T(8,128)S(1)}) custom-call(s32[1,6]{1,0:T(1,128)} %refs_0_.7, s32[1,6]{1,0:T(1,128)} %refs_1_.7, s32[1]{0:T(128)S(6)} %copy.30.refs_2_, bf16[1,6,4,512,512]{4,3,2,1,0:T(8,128)(2,1)} %refs_3_.7, bf16[32,512,256]{2,1,0:T(8,128)(2,1)} %refs_4_.6, ...), custom_call_target="tpu_custom_call" | custom-call | flops 1610612736 | bytes 10485760 | tf_op jit(solution)/shard_map/pallas_call | solution.py:158
  17.8 4.4 %collective-permute-start = (f32[1,512,256]{2,1,0:T(8,128)S(1)}, f32[1,512,256]{2,1,0:T(8,128)S(1)}, u32[]{:S(2)}, u32[]{:S(2)}) collective-permute-start(f32[1,512,256]{2,1,0:T(8,128)S(1)} %get-tuple-element.36), channel_id=1, source_target_pairs={{2,4},{4,2},{3,5},{5,3},{10,12},{12,10},{11,13},{13,11},{18,20},{2... | collective-permute-start | bytes 1572872 | tf_op jit(solution)/shard_map/ppermute | solution.py:294
  22.2 0.0 collective-permute-done.2.arrived
  22.2 0.0 collective-permute-done.1.core_in
  22.2 0.1 shard_map.76
  22.3 0.1 collective-permute-start.3
  22.4 0.1 collective-permute-start.4
  22.5 2.6 %collective-permute-done.5.arrived = f32[1,512,256]{2,1,0:T(8,128)S(1)} collective-permute-done((f32[1,512,256]{2,1,0:T(8,128)S(1)}, f32[1,512,256]{2,1,0:T(8,128)S(1)}, u32[]{:S(2)}, u32[]{:S(2)}) %collective-permute-start.5) | collective-permute-done | bytes 524320 | tf_op jit(solution)/shard_map/ppermute | solution.py:292
  25.1 0.1 shard_map.79
  25.2 1.9 %collective-permute-start.6 = (f32[1,512,256]{2,1,0:T(8,128)S(1)}, f32[1,512,256]{2,1,0:T(8,128)S(1)}, u32[]{:S(2)}, u32[]{:S(2)}) collective-permute-start(f32[1,512,256]{2,1,0:T(8,128)S(1)} %get-tuple-element.44), channel_id=1, source_target_pairs={{1,2},{2,1},{3,4},{4,3},{5,6},{6,5},{9,10},{10,9},{11,12},{12,11},... | collective-permute-start | bytes 1572872 | tf_op jit(solution)/shard_map/ppermute | solution.py:299
  27.1 2.9 %collective-permute-start.7 = (f32[1,512,256]{2,1,0:T(8,128)S(1)}, f32[1,512,256]{2,1,0:T(8,128)S(1)}, u32[]{:S(2)}, u32[]{:S(2)}) collective-permute-start(f32[1,512,256]{2,1,0:T(8,128)S(1)} %get-tuple-element.45), channel_id=1, source_target_pairs={{8,16},{16,8},{9,17},{17,9},{10,18},{18,10},{11,19},{19,11},{12,20... | collective-permute-start | bytes 1572872 | tf_op jit(solution)/shard_map/ppermute | solution.py:300
  30.0 4.9 %shard_map.81 = (f32[3,512,256]{2,1,0:T(8,128)S(1)}, f32[3,512,256]{2,1,0:T(8,128)S(1)}, f32[1,512,256]{2,1,0:T(8,128)S(1)}, f32[1,512,256]{2,1,0:T(8,128)S(1)},...) custom-call(s32[1,6]{1,0:T(1,128)} %refs_0_.7, s32[1,6]{1,0:T(1,128)} %refs_1_.7, ...), custom_call_target="tpu_custom_call" | custom-call | flops 1610612736 | bytes 10485760 | tf_op jit(solution)/shard_map/pallas_call | solution.py:158
  34.9 0.0 collective-permute-done.arrived
  34.9 0.1 shard_map.75.refs_0_
  35.0 0.7 collective-permute-done.3.refs_1_
  35.7 0.1 shard_map.77.refs_0_
  35.7 0.0 copy-start
  35.7 0.0 copy-start.1
  35.7 0.0 collective-permute-done.4.refs_1_
  35.8 0.1 shard_map.78.refs_0_
  35.8 6.8 %collective-permute-done.6.refs_1_ = f32[1,512,256]{2,1,0:T(8,128)S(1)} collective-permute-done((f32[1,512,256]{2,1,0:T(8,128)S(1)}, f32[1,512,256]{2,1,0:T(8,128)S(1)}, u32[]{:S(2)}, u32[]{:S(2)}) %collective-permute-start.6) | collective-permute-done | bytes 524320 | tf_op jit(solution)/shard_map/ppermute | solution.py:299
  42.6 0.1 shard_map.80.refs_6_
  42.6 0.0 collective-permute-done.7.refs_7_
  42.6 0.0 copy-done
  42.7 0.0 copy-done.1
  42.7 1.1 %shard_map.82 = (f32[3,512,256]{2,1,0:T(8,128)S(1)}, f32[3,512,256]{2,1,0:T(8,128)S(1)}, f32[1,512,256]{2,1,0:T(8,128)S(1)}, f32[1,512,256]{2,1,0:T(8,128)S(1)},...) custom-call(s32[1,6]{1,0:T(1,128)} %refs_0_.7, ...), custom_call_target="tpu_custom_call", output_to_operand_aliasing={{0}: (8, {}), {1}: (9, {}), {2}: (10, {}), {3}: (11, {}), {... | custom-call | flops 134217728 | bytes 2097152 | tf_op jit(solution)/shard_map/pallas_call | solution.py:222
  43.8 0.1 collective-permute-start.9
  43.9 3.1 %collective-permute-start.10 = (f32[1,512,256]{2,1,0:T(8,128)S(1)}, f32[1,512,256]{2,1,0:T(8,128)S(1)}, u32[]{:S(2)}, u32[]{:S(2)}) collective-permute-start(f32[1,512,256]{2,1,0:T(8,128)S(1)} %get-tuple-element.56), channel_id=1, source_target_pairs={{8,16},{16,8},{9,17},{17,9},{10,18},{18,10},{11,19},{19,11},{12,20... | collective-permute-start | bytes 1572872 | tf_op jit(solution)/shard_map/ppermute | solution.py:291
  47.0 2.5 %collective-permute-start.13 = (f32[1,512,256]{2,1,0:T(8,128)S(1)}, f32[1,512,256]{2,1,0:T(8,128)S(1)}, u32[]{:S(2)}, u32[]{:S(2)}) collective-permute-start(f32[1,512,256]{2,1,0:T(8,128)S(1)} %get-tuple-element.60), channel_id=1, source_target_pairs={{8,16},{16,8},{9,17},{17,9},{10,18},{18,10},{11,19},{19,11},{12,20... | collective-permute-start | bytes 1572872 | tf_op jit(solution)/shard_map/ppermute | solution.py:292
  49.5 3.3 %collective-permute-start.8 = (f32[1,512,256]{2,1,0:T(8,128)S(1)}, f32[1,512,256]{2,1,0:T(8,128)S(1)}, u32[]{:S(2)}, u32[]{:S(2)}) collective-permute-start(f32[1,512,256]{2,1,0:T(8,128)S(1)} %get-tuple-element.53), channel_id=1, source_target_pairs={{2,4},{4,2},{3,5},{5,3},{10,12},{12,10},{11,13},{13,11},{18,20},{2... | collective-permute-start | bytes 1572872 | tf_op jit(solution)/shard_map/ppermute | solution.py:294
  52.8 1.9 %collective-permute-done.10.arrived = f32[1,512,256]{2,1,0:T(8,128)S(1)} collective-permute-done((f32[1,512,256]{2,1,0:T(8,128)S(1)}, f32[1,512,256]{2,1,0:T(8,128)S(1)}, u32[]{:S(2)}, u32[]{:S(2)}) %collective-permute-start.10) | collective-permute-done | bytes 524320 | tf_op jit(solution)/shard_map/ppermute | solution.py:291
  54.7 0.0 collective-permute-done.9.core_in
  54.7 0.1 shard_map.84
  54.8 0.1 collective-permute-start.11
  54.8 1.2 %collective-permute-start.12 = (f32[1,512,256]{2,1,0:T(8,128)S(1)}, f32[1,512,256]{2,1,0:T(8,128)S(1)}, u32[]{:S(2)}, u32[]{:S(2)}) collective-permute-start(f32[1,512,256]{2,1,0:T(8,128)S(1)} %get-tuple-element.59), channel_id=1, source_target_pairs={{0,2},{2,0},{1,3},{3,1},{4,6},{6,4},{5,7},{7,5},{8,10},{10,8},{9,1... | collective-permute-start | bytes 1572872 | tf_op jit(solution)/shard_map/ppermute | solution.py:297
  56.1 4.2 %collective-permute-done.13.arrived = f32[1,512,256]{2,1,0:T(8,128)S(1)} collective-permute-done((f32[1,512,256]{2,1,0:T(8,128)S(1)}, f32[1,512,256]{2,1,0:T(8,128)S(1)}, u32[]{:S(2)}, u32[]{:S(2)}) %collective-permute-start.13) | collective-permute-done | bytes 524320 | tf_op jit(solution)/shard_map/ppermute | solution.py:292
  60.3 0.1 shard_map.87
  60.4 2.9 %collective-permute-start.14 = (f32[1,512,256]{2,1,0:T(8,128)S(1)}, f32[1,512,256]{2,1,0:T(8,128)S(1)}, u32[]{:S(2)}, u32[]{:S(2)}) collective-permute-start(f32[1,512,256]{2,1,0:T(8,128)S(1)} %get-tuple-element.62), channel_id=1, source_target_pairs={{1,2},{2,1},{3,4},{4,3},{5,6},{6,5},{9,10},{10,9},{11,12},{12,11},... | collective-permute-start | bytes 1572872 | tf_op jit(solution)/shard_map/ppermute | solution.py:299
  63.3 1.9 %collective-permute-start.15 = (f32[1,512,256]{2,1,0:T(8,128)S(1)}, f32[1,512,256]{2,1,0:T(8,128)S(1)}, u32[]{:S(2)}, u32[]{:S(2)}) collective-permute-start(f32[1,512,256]{2,1,0:T(8,128)S(1)} %get-tuple-element.63), channel_id=1, source_target_pairs={{8,16},{16,8},{9,17},{17,9},{10,18},{18,10},{11,19},{19,11},{12,20... | collective-permute-start | bytes 1572872 | tf_op jit(solution)/shard_map/ppermute | solution.py:300
  65.2 0.2 collective-permute-done.8.arrived
  65.4 0.1 shard_map.83.refs_0_
  65.4 8.3 %collective-permute-done.11.refs_1_ = f32[1,512,256]{2,1,0:T(8,128)S(1)} collective-permute-done((f32[1,512,256]{2,1,0:T(8,128)S(1)}, f32[1,512,256]{2,1,0:T(8,128)S(1)}, u32[]{:S(2)}, u32[]{:S(2)}) %collective-permute-start.11) | collective-permute-done | bytes 524320 | tf_op jit(solution)/shard_map/ppermute | solution.py:296
  73.7 0.1 shard_map.85.refs_0_
  73.8 0.0 collective-permute-done.12.refs_1_
  73.8 0.1 shard_map.86.refs_0_
  73.9 2.5 %collective-permute-done.14.refs_1_ = f32[1,512,256]{2,1,0:T(8,128)S(1)} collective-permute-done((f32[1,512,256]{2,1,0:T(8,128)S(1)}, f32[1,512,256]{2,1,0:T(8,128)S(1)}, u32[]{:S(2)}, u32[]{:S(2)}) %collective-permute-start.14) | collective-permute-done | bytes 524320 | tf_op jit(solution)/shard_map/ppermute | solution.py:299
  76.4 0.1 shard_map.88.refs_0_
  76.4 0.0 collective-permute-done.15.refs_1_
  76.5 1.1 %shard_map.89 = bf16[2,512,256]{2,1,0:T(8,128)(2,1)} custom-call(bf16[1,512,512]{2,1,0:T(8,128)(2,1)S(1)} %copy-done, bf16[2,512,256]{2,1,0:T(8,128)(2,1)S(1)} %copy-done.1, f32[1,512,256]{2,1,0:T(8,128)S(1)} %shard_map.88.refs_0_, f32[1,512,256]{2,1,0:T(8,128)S(1)} %collective-permute-done.15.refs_1_, bf16[512,256]{1,0:T(8,128)(2,1)S(1)} %get-tuple-element.64.refs_2_), custom_call_target="tpu_custom_call" | custom-call | tf_op jit(solution)/shard_map/pallas_call | solution.py:255
Async XLA Ops:
  4.4 17.8 %collective-permute-start.1 = (f32[3,512,256]{2,1,0:T(8,128)S(1)}, f32[3,512,256]{2,1,0:T(8,128)S(1)}, u32[]{:S(2)}, u32[]{:S(2)}) collective-permute-start(f32[3,512,256]{2,1,0:T(8,128)S(1)} %get-tuple-element.35.refs_5_), channel_id=1, source_target_pairs={{0,8},{8,0},{16,24},{24,16},{1,9},{9,1},{17,25},{25,17},{2,10},{10... | collective-permute-start | bytes 4718600 | tf_op jit(solution)/shard_map/ppermute | solution.py:293
  8.7 13.5 %collective-permute-start.2 = (f32[1,512,256]{2,1,0:T(8,128)S(1)}, f32[1,512,256]{2,1,0:T(8,128)S(1)}, u32[]{:S(2)}, u32[]{:S(2)}) collective-permute-start(f32[1,512,256]{2,1,0:T(8,128)S(1)} %get-tuple-element.38), channel_id=1, source_target_pairs={{8,16},{16,8},{9,17},{17,9},{10,18},{18,10},{11,19},{19,11},{12,20... | collective-permute-start | bytes 1572872 | tf_op jit(solution)/shard_map/ppermute | solution.py:291
  10.6 14.5 %collective-permute-start.5 = (f32[1,512,256]{2,1,0:T(8,128)S(1)}, f32[1,512,256]{2,1,0:T(8,128)S(1)}, u32[]{:S(2)}, u32[]{:S(2)}) collective-permute-start(f32[1,512,256]{2,1,0:T(8,128)S(1)} %get-tuple-element.42), channel_id=1, source_target_pairs={{8,16},{16,8},{9,17},{17,9},{10,18},{18,10},{11,19},{19,11},{12,20... | collective-permute-start | bytes 1572872 | tf_op jit(solution)/shard_map/ppermute | solution.py:292
  17.8 17.1 %collective-permute-start = (f32[1,512,256]{2,1,0:T(8,128)S(1)}, f32[1,512,256]{2,1,0:T(8,128)S(1)}, u32[]{:S(2)}, u32[]{:S(2)}) collective-permute-start(f32[1,512,256]{2,1,0:T(8,128)S(1)} %get-tuple-element.36), channel_id=1, source_target_pairs={{2,4},{4,2},{3,5},{5,3},{10,12},{12,10},{11,13},{13,11},{18,20},{2... | collective-permute-start | bytes 1572872 | tf_op jit(solution)/shard_map/ppermute | solution.py:294
  22.3 13.4 %collective-permute-start.3 = (f32[1,512,256]{2,1,0:T(8,128)S(1)}, f32[1,512,256]{2,1,0:T(8,128)S(1)}, u32[]{:S(2)}, u32[]{:S(2)}) collective-permute-start(f32[1,512,256]{2,1,0:T(8,128)S(1)} %get-tuple-element.40), channel_id=1, source_target_pairs={{0,1},{1,0},{2,3},{3,2},{4,5},{5,4},{6,7},{7,6},{8,9},{9,8},{10,11... | collective-permute-start | bytes 1572872 | tf_op jit(solution)/shard_map/ppermute | solution.py:296
  22.4 13.4 %collective-permute-start.4 = (f32[1,512,256]{2,1,0:T(8,128)S(1)}, f32[1,512,256]{2,1,0:T(8,128)S(1)}, u32[]{:S(2)}, u32[]{:S(2)}) collective-permute-start(f32[1,512,256]{2,1,0:T(8,128)S(1)} %get-tuple-element.41), channel_id=1, source_target_pairs={{0,2},{2,0},{1,3},{3,1},{4,6},{6,4},{5,7},{7,5},{8,10},{10,8},{9,1... | collective-permute-start | bytes 1572872 | tf_op jit(solution)/shard_map/ppermute | solution.py:297
  25.2 17.4 %collective-permute-start.6 = (f32[1,512,256]{2,1,0:T(8,128)S(1)}, f32[1,512,256]{2,1,0:T(8,128)S(1)}, u32[]{:S(2)}, u32[]{:S(2)}) collective-permute-start(f32[1,512,256]{2,1,0:T(8,128)S(1)} %get-tuple-element.44), channel_id=1, source_target_pairs={{1,2},{2,1},{3,4},{4,3},{5,6},{6,5},{9,10},{10,9},{11,12},{12,11},... | collective-permute-start | bytes 1572872 | tf_op jit(solution)/shard_map/ppermute | solution.py:299
  27.1 15.5 %collective-permute-start.7 = (f32[1,512,256]{2,1,0:T(8,128)S(1)}, f32[1,512,256]{2,1,0:T(8,128)S(1)}, u32[]{:S(2)}, u32[]{:S(2)}) collective-permute-start(f32[1,512,256]{2,1,0:T(8,128)S(1)} %get-tuple-element.45), channel_id=1, source_target_pairs={{8,16},{16,8},{9,17},{17,9},{10,18},{18,10},{11,19},{19,11},{12,20... | collective-permute-start | bytes 1572872 | tf_op jit(solution)/shard_map/ppermute | solution.py:300
  35.7 6.9 %copy-start = (bf16[1,512,512]{2,1,0:T(8,128)(2,1)S(1)}, bf16[1,512,512]{2,1,0:T(8,128)(2,1)}, u32[]{:S(2)}) copy-start(bf16[1,512,512]{2,1,0:T(8,128)(2,1)} %inverse.1) | copy-start | bytes 1572868
  35.7 6.9 %copy-start.1 = (bf16[2,512,256]{2,1,0:T(8,128)(2,1)S(1)}, bf16[2,512,256]{2,1,0:T(8,128)(2,1)}, u32[]{:S(2)}) copy-start(bf16[2,512,256]{2,1,0:T(8,128)(2,1)} %incident.1) | copy-start | bytes 1572868
  43.8 10.9 %collective-permute-start.9 = (f32[3,512,256]{2,1,0:T(8,128)S(1)}, f32[3,512,256]{2,1,0:T(8,128)S(1)}, u32[]{:S(2)}, u32[]{:S(2)}) collective-permute-start(f32[3,512,256]{2,1,0:T(8,128)S(1)} %get-tuple-element.55), channel_id=1, source_target_pairs={{0,8},{8,0},{16,24},{24,16},{1,9},{9,1},{17,25},{25,17},{2,10},{10... | collective-permute-start | bytes 4718600 | tf_op jit(solution)/shard_map/ppermute | solution.py:293
  43.9 10.8 %collective-permute-start.10 = (f32[1,512,256]{2,1,0:T(8,128)S(1)}, f32[1,512,256]{2,1,0:T(8,128)S(1)}, u32[]{:S(2)}, u32[]{:S(2)}) collective-permute-start(f32[1,512,256]{2,1,0:T(8,128)S(1)} %get-tuple-element.56), channel_id=1, source_target_pairs={{8,16},{16,8},{9,17},{17,9},{10,18},{18,10},{11,19},{19,11},{12,20... | collective-permute-start | bytes 1572872 | tf_op jit(solution)/shard_map/ppermute | solution.py:291
  47.0 13.3 %collective-permute-start.13 = (f32[1,512,256]{2,1,0:T(8,128)S(1)}, f32[1,512,256]{2,1,0:T(8,128)S(1)}, u32[]{:S(2)}, u32[]{:S(2)}) collective-permute-start(f32[1,512,256]{2,1,0:T(8,128)S(1)} %get-tuple-element.60), channel_id=1, source_target_pairs={{8,16},{16,8},{9,17},{17,9},{10,18},{18,10},{11,19},{19,11},{12,20... | collective-permute-start | bytes 1572872 | tf_op jit(solution)/shard_map/ppermute | solution.py:292
  49.5 15.9 %collective-permute-start.8 = (f32[1,512,256]{2,1,0:T(8,128)S(1)}, f32[1,512,256]{2,1,0:T(8,128)S(1)}, u32[]{:S(2)}, u32[]{:S(2)}) collective-permute-start(f32[1,512,256]{2,1,0:T(8,128)S(1)} %get-tuple-element.53), channel_id=1, source_target_pairs={{2,4},{4,2},{3,5},{5,3},{10,12},{12,10},{11,13},{13,11},{18,20},{2... | collective-permute-start | bytes 1572872 | tf_op jit(solution)/shard_map/ppermute | solution.py:294
  54.8 19.0 %collective-permute-start.11 = (f32[1,512,256]{2,1,0:T(8,128)S(1)}, f32[1,512,256]{2,1,0:T(8,128)S(1)}, u32[]{:S(2)}, u32[]{:S(2)}) collective-permute-start(f32[1,512,256]{2,1,0:T(8,128)S(1)} %get-tuple-element.58), channel_id=1, source_target_pairs={{0,1},{1,0},{2,3},{3,2},{4,5},{5,4},{6,7},{7,6},{8,9},{9,8},{10,11... | collective-permute-start | bytes 1572872 | tf_op jit(solution)/shard_map/ppermute | solution.py:296
  54.8 18.9 %collective-permute-start.12 = (f32[1,512,256]{2,1,0:T(8,128)S(1)}, f32[1,512,256]{2,1,0:T(8,128)S(1)}, u32[]{:S(2)}, u32[]{:S(2)}) collective-permute-start(f32[1,512,256]{2,1,0:T(8,128)S(1)} %get-tuple-element.59), channel_id=1, source_target_pairs={{0,2},{2,0},{1,3},{3,1},{4,6},{6,4},{5,7},{7,5},{8,10},{10,8},{9,1... | collective-permute-start | bytes 1572872 | tf_op jit(solution)/shard_map/ppermute | solution.py:297
  60.4 16.0 %collective-permute-start.14 = (f32[1,512,256]{2,1,0:T(8,128)S(1)}, f32[1,512,256]{2,1,0:T(8,128)S(1)}, u32[]{:S(2)}, u32[]{:S(2)}) collective-permute-start(f32[1,512,256]{2,1,0:T(8,128)S(1)} %get-tuple-element.62), channel_id=1, source_target_pairs={{1,2},{2,1},{3,4},{4,3},{5,6},{6,5},{9,10},{10,9},{11,12},{12,11},... | collective-permute-start | bytes 1572872 | tf_op jit(solution)/shard_map/ppermute | solution.py:299
  63.3 13.2 %collective-permute-start.15 = (f32[1,512,256]{2,1,0:T(8,128)S(1)}, f32[1,512,256]{2,1,0:T(8,128)S(1)}, u32[]{:S(2)}, u32[]{:S(2)}) collective-permute-start(f32[1,512,256]{2,1,0:T(8,128)S(1)} %get-tuple-element.63), channel_id=1, source_target_pairs={{8,16},{16,8},{9,17},{17,9},{10,18},{18,10},{11,19},{19,11},{12,20... | collective-permute-start | bytes 1572872 | tf_op jit(solution)/shard_map/ppermute | solution.py:300

commit v3 on v2

--- a/solution.py
+++ b/solution.py
@@ -178,11 +178,16 @@
 
 def march_kernel(*refs):
     n = len(PAYLOADS)
-    meta, (couplings, inverse, incident), terms = refs[:3], refs[3:6], refs[6:8]
+    meta, (couplings, inverse_hbm, incident_hbm), terms = refs[:3], refs[3:6], refs[6:8]
     outs = refs[8 + n : 8 + 2 * n]
     current = refs[8 + 2 * n]
-    targets, delays, counts, weights, held, in_sems, sem, sems = refs[9 + 2 * n :]
-    for copy in fetch(meta, (targets, delays, counts), sems):
+    targets, delays, counts, inverse, incident, weights, held, in_sems, sem, sems = refs[9 + 2 * n :]
+    sources = (*meta, incident_hbm.at[0], inverse_hbm.at[0])
+    copies = fetch(sources, (targets, delays, counts, incident, inverse), sems)
+    field = terms[0][0] + terms[1][0]
+    copies[3].wait()
+    right = (incident[...].astype(jnp.float32) - field).astype(jnp.bfloat16)
+    for copy in copies[:3]:
         copy.wait()
     slots = targets.shape[1]
     at, useful = places(targets)
@@ -191,9 +196,8 @@
         @pl.when(fresh[c])
         def _(c=c):
             pltpu.make_async_copy(couplings.at[0, c, 0], weights.at[c], in_sems.at[c]).start()
-    field = terms[0][0] + terms[1][0]
-    right = (incident[0].astype(jnp.float32) - field).astype(jnp.bfloat16)
-    current[...] = jnp.dot(inverse[0], right, preferred_element_type=jnp.float32).astype(jnp.bfloat16)
+    copies[4].wait()
+    current[...] = jnp.dot(inverse[...], right, preferred_element_type=jnp.float32).astype(jnp.bfloat16)
     for c in range(slots):
         @pl.when(fresh[c])
         def _(c=c):
@@ -223,22 +227,24 @@
         march_kernel,
         out_shape=[jax.ShapeDtypeStruct(p.shape, p.dtype) for p in payloads]
         + [jax.ShapeDtypeStruct((unknowns, width), jnp.bfloat16)],
-        in_specs=[pl.BlockSpec(memory_space=pl.ANY)] * 4 + [vmem] * 4 + [hbm] * n,
+        in_specs=[pl.BlockSpec(memory_space=pl.ANY)] * 6 + [vmem] * 2 + [hbm] * n,
         out_specs=[hbm] * n + [vmem],
         input_output_aliases={8 + i: i for i in range(n)},
         scratch_shapes=[
             pltpu.SMEM(targets.shape, jnp.int32),
             pltpu.SMEM(delays.shape, jnp.int32),
             pltpu.SMEM(counts.shape, jnp.int32),
+            pltpu.VMEM((unknowns, unknowns), jnp.bfloat16),
+            pltpu.VMEM((unknowns, width), jnp.bfloat16),
             pltpu.VMEM((slots, unknowns, unknowns), jnp.bfloat16),
             pltpu.VMEM((unknowns, width), jnp.float32),
             pltpu.SemaphoreType.DMA((slots,)),
             pltpu.SemaphoreType.DMA,
-            pltpu.SemaphoreType.DMA((3,)),
+            pltpu.SemaphoreType.DMA((5,)),
         ],
         compiler_params=pltpu.CompilerParams(vmem_limit_bytes=24 * 2**20),
         cost_estimate=pl.CostEstimate(flops=2 * unknowns * unknowns * width, bytes_accessed=2**21, transcendentals=0),
-    )(in_hbm(targets), in_hbm(delays), counts, in_hbm(couplings), inverse, incident, *sums, *payloads)
+    )(in_hbm(targets), in_hbm(delays), counts, in_hbm(couplings), in_hbm(inverse), in_hbm(incident), *sums, *payloads)
     return current, updated
 
 
@@ -275,7 +281,7 @@
     )(*operands, *carried)
 
 
-def join_kernel(row, arrived, near, core_in, *refs):
+def join_kernel(row, arrived, core_in, near, *refs):
     total = refs[len(refs) // 2]
     total[0] = arrived[0] + near[row] + core_in[row]
 
@@ -292,13 +298,13 @@
     skew_in = lax.ppermute(cross_skew, "group", x_pairs)
     core_in = lax.ppermute(core, "group", swap_pairs(groups, 0))
     za_in = lax.ppermute(za, ("group", "dev"), far_pairs(groups, devs, 0))
-    y, zb = stage(functools.partial(join_kernel, 0), (y_in, near, core_in), (zb,))
+    y, zb = stage(functools.partial(join_kernel, 0), (y_in, core_in, near), (zb,))
     y_in = lax.ppermute(y, "dev", swap_pairs(devs, 0))
     zb_in = lax.ppermute(zb, ("group", "dev"), far_pairs(groups, devs, 1))
-    skew, cross_own = stage(functools.partial(join_kernel, 1), (skew_in, near, core_in), (cross_own,))
+    skew, cross_own = stage(functools.partial(join_kernel, 1), (skew_in, core_in, near), (cross_own,))
     skew_in = lax.ppermute(skew, "dev", swap_pairs(devs, 1))
     own_in = lax.ppermute(cross_own, "group", x_pairs)
-    (field,) = stage(functools.partial(join_kernel, 2), (za_in, near, core_in))
+    (field,) = stage(functools.partial(join_kernel, 2), (za_in, core_in, near))
     (field,) = stage(sum_kernel, (field, y_in))
     (field,) = stage(sum_kernel, (field, zb_in))
     (field,) = stage(sum_kernel, (field, skew_in))

time: 77.3 us -> 77.6 us (level)
  the two profiles are of different devices: /device:TPU:9 before, /device:TPU:13 now
where the time goes in v3:
time: 77.6 us; the launch traced here: 77.2 us
  starting transfers between devices  32.6 us (42%)
  waiting for transfers between devices  27 us (35%)
  Pallas kernels  15.7 us (20%)
  local copies, waits for them, and re-layouts  1.03 us (1%)
  between operations  0.95 us (1%)
    ppermute x2, waiting for transfers between devices, deliver(): y_in = lax.ppermute(y, 'dev', swap_pairs(devs, 0))  17 us
    pallas_call x3, Pallas kernels, slot_terms(): pl.pallas_call(functools.partial(slot_kernel, shift, parts, len(earlier))...  12.1 us
    ppermute x2, waiting for transfers between devices, deliver(): skew_in = lax.ppermute(cross_skew, 'group', x_pairs)  8.11 us
    ppermute x2, starting transfers between devices, deliver(): skew_in = lax.ppermute(cross_skew, 'group', x_pairs)  7.18 us
    ppermute x2, starting transfers between devices, deliver(): own_in = lax.ppermute(cross_own, 'group', x_pairs)  6.79 us
    ppermute x2, starting transfers between devices, deliver(): za_in = lax.ppermute(za, ('group', 'dev'), far_pairs(groups, devs, 0))  5.21 us
    ppermute x2, starting transfers between devices, deliver(): skew_in = lax.ppermute(skew, 'dev', swap_pairs(devs, 1))  4.18 us
    ppermute x2, starting transfers between devices, deliver(): y_in = lax.ppermute(cross_y, 'group', x_pairs)  3.93 us
  transfers between devices with their start and end apart: 16, of which 5 were waited for; matrix products, arithmetic and copies ran while one was open for 0% of the time, Pallas kernels for 12%

profile of v3, /device:TPU:13, one launch (start us, length us, event | category | flops | bytes accessed | tf_op | source)
XLA Modules:
  0.0 77.2 jit_solution(12859749989952451392)
XLA Ops:
  0.7 3.7 %shard_map.73 = (f32[3,512,256]{2,1,0:T(8,128)S(1)}, f32[3,512,256]{2,1,0:T(8,128)S(1)}, f32[1,512,256]{2,1,0:T(8,128)S(1)}, f32[1,512,256]{2,1,0:T(8,128)S(1)}) custom-call(s32[1,6]{1,0:T(1,128)} %refs_0_.7, s32[1,6]{1,0:T(1,128)} %refs_1_.7, s32[1]{0:T(128)S(6)} %copy.30.refs_2_, bf16[1,6,4,512,512]{4,3,2,1,0:T(8,128)(2,1)} %refs_3_.7, ...), custom_call_target="tpu_custom_call" | custom-call | flops 1610612736 | bytes 10485760 | tf_op jit(solution)/shard_map/pallas_call | solution.py:158
  4.4 2.5 %collective-permute-start.1 = (f32[3,512,256]{2,1,0:T(8,128)S(1)}, f32[3,512,256]{2,1,0:T(8,128)S(1)}, u32[]{:S(2)}, u32[]{:S(2)}) collective-permute-start(f32[3,512,256]{2,1,0:T(8,128)S(1)} %get-tuple-element.35.refs_5_), channel_id=1, source_target_pairs={{0,8},{8,0},{16,24},{24,16},{1,9},{9,1},{17,25},{25,17},{2,10},{10... | collective-permute-start | bytes 4718600 | tf_op jit(solution)/shard_map/ppermute | solution.py:299
  6.9 1.9 %collective-permute-start.2 = (f32[1,512,256]{2,1,0:T(8,128)S(1)}, f32[1,512,256]{2,1,0:T(8,128)S(1)}, u32[]{:S(2)}, u32[]{:S(2)}) collective-permute-start(f32[1,512,256]{2,1,0:T(8,128)S(1)} %get-tuple-element.38), channel_id=1, source_target_pairs={{8,16},{16,8},{9,17},{17,9},{10,18},{18,10},{11,19},{19,11},{12,20... | collective-permute-start | bytes 1572872 | tf_op jit(solution)/shard_map/ppermute | solution.py:297
  8.9 3.6 %collective-permute-start.5 = (f32[1,512,256]{2,1,0:T(8,128)S(1)}, f32[1,512,256]{2,1,0:T(8,128)S(1)}, u32[]{:S(2)}, u32[]{:S(2)}) collective-permute-start(f32[1,512,256]{2,1,0:T(8,128)S(1)} %get-tuple-element.42), channel_id=1, source_target_pairs={{8,16},{16,8},{9,17},{17,9},{10,18},{18,10},{11,19},{19,11},{12,20... | collective-permute-start | bytes 1572872 | tf_op jit(solution)/shard_map/ppermute | solution.py:298
  12.5 3.6 %shard_map.74 = (f32[1,512,256]{2,1,0:T(8,128)S(1)}, f32[1,512,256]{2,1,0:T(8,128)S(1)}, f32[1,512,256]{2,1,0:T(8,128)S(1)}) custom-call(s32[1,6]{1,0:T(1,128)} %refs_0_.7, s32[1,6]{1,0:T(1,128)} %refs_1_.7, s32[1]{0:T(128)S(6)} %copy.30.refs_2_, bf16[1,6,4,512,512]{4,3,2,1,0:T(8,128)(2,1)} %refs_3_.7, bf16[32,512,256]{2,1,0:T(8,128)(2,1)} %refs_4_.6, ...), custom_call_target="tpu_custom_call" | custom-call | flops 1610612736 | bytes 10485760 | tf_op jit(solution)/shard_map/pallas_call | solution.py:158
  16.1 1.9 %collective-permute-start = (f32[1,512,256]{2,1,0:T(8,128)S(1)}, f32[1,512,256]{2,1,0:T(8,128)S(1)}, u32[]{:S(2)}, u32[]{:S(2)}) collective-permute-start(f32[1,512,256]{2,1,0:T(8,128)S(1)} %get-tuple-element.36), channel_id=1, source_target_pairs={{2,4},{4,2},{3,5},{5,3},{10,12},{12,10},{11,13},{13,11},{18,20},{2... | collective-permute-start | bytes 1572872 | tf_op jit(solution)/shard_map/ppermute | solution.py:300
  18.0 0.0 collective-permute-done.2.arrived
  18.0 0.0 collective-permute-done.1.core_in
  18.0 0.1 shard_map.76
  18.1 1.2 %collective-permute-start.3 = (f32[1,512,256]{2,1,0:T(8,128)S(1)}, f32[1,512,256]{2,1,0:T(8,128)S(1)}, u32[]{:S(2)}, u32[]{:S(2)}) collective-permute-start(f32[1,512,256]{2,1,0:T(8,128)S(1)} %get-tuple-element.40), channel_id=1, source_target_pairs={{0,1},{1,0},{2,3},{3,2},{4,5},{5,4},{6,7},{7,6},{8,9},{9,8},{10,11... | collective-permute-start | bytes 1572872 | tf_op jit(solution)/shard_map/ppermute | solution.py:302
  19.3 0.0 collective-permute-start.4
  19.3 4.1 %collective-permute-done.5.arrived = f32[1,512,256]{2,1,0:T(8,128)S(1)} collective-permute-done((f32[1,512,256]{2,1,0:T(8,128)S(1)}, f32[1,512,256]{2,1,0:T(8,128)S(1)}, u32[]{:S(2)}, u32[]{:S(2)}) %collective-permute-start.5) | collective-permute-done | bytes 524320 | tf_op jit(solution)/shard_map/ppermute | solution.py:298
  23.3 0.1 shard_map.79
  23.4 2.2 %collective-permute-start.6 = (f32[1,512,256]{2,1,0:T(8,128)S(1)}, f32[1,512,256]{2,1,0:T(8,128)S(1)}, u32[]{:S(2)}, u32[]{:S(2)}) collective-permute-start(f32[1,512,256]{2,1,0:T(8,128)S(1)} %get-tuple-element.44), channel_id=1, source_target_pairs={{1,2},{2,1},{3,4},{4,3},{5,6},{6,5},{9,10},{10,9},{11,12},{12,11},... | collective-permute-start | bytes 1572872 | tf_op jit(solution)/shard_map/ppermute | solution.py:305
  25.7 3.0 %collective-permute-start.7 = (f32[1,512,256]{2,1,0:T(8,128)S(1)}, f32[1,512,256]{2,1,0:T(8,128)S(1)}, u32[]{:S(2)}, u32[]{:S(2)}) collective-permute-start(f32[1,512,256]{2,1,0:T(8,128)S(1)} %get-tuple-element.45), channel_id=1, source_target_pairs={{8,16},{16,8},{9,17},{17,9},{10,18},{18,10},{11,19},{19,11},{12,20... | collective-permute-start | bytes 1572872 | tf_op jit(solution)/shard_map/ppermute | solution.py:306
  28.7 4.9 %shard_map.81 = (f32[3,512,256]{2,1,0:T(8,128)S(1)}, f32[3,512,256]{2,1,0:T(8,128)S(1)}, f32[1,512,256]{2,1,0:T(8,128)S(1)}, f32[1,512,256]{2,1,0:T(8,128)S(1)},...) custom-call(s32[1,6]{1,0:T(1,128)} %refs_0_.7, s32[1,6]{1,0:T(1,128)} %refs_1_.7, ...), custom_call_target="tpu_custom_call" | custom-call | flops 1610612736 | bytes 10485760 | tf_op jit(solution)/shard_map/pallas_call | solution.py:158
  33.6 0.0 collective-permute-done.arrived
  33.6 0.1 shard_map.75.refs_0_
  33.7 8.3 %collective-permute-done.3.refs_1_ = f32[1,512,256]{2,1,0:T(8,128)S(1)} collective-permute-done((f32[1,512,256]{2,1,0:T(8,128)S(1)}, f32[1,512,256]{2,1,0:T(8,128)S(1)}, u32[]{:S(2)}, u32[]{:S(2)}) %collective-permute-start.3) | collective-permute-done | bytes 524320 | tf_op jit(solution)/shard_map/ppermute | solution.py:302
  41.9 0.1 shard_map.77.refs_0_
  42.0 0.0 collective-permute-done.4.refs_1_
  42.0 0.1 shard_map.78.refs_0_
  42.1 0.0 collective-permute-done.6.refs_1_
  42.1 0.1 shard_map.80.refs_6_
  42.2 0.0 collective-permute-done.7.refs_7_
  42.2 1.6 %shard_map.82 = (f32[3,512,256]{2,1,0:T(8,128)S(1)}, f32[3,512,256]{2,1,0:T(8,128)S(1)}, f32[1,512,256]{2,1,0:T(8,128)S(1)}, f32[1,512,256]{2,1,0:T(8,128)S(1)},...) custom-call(s32[1,6]{1,0:T(1,128)} %refs_0_.7, ...), custom_call_target="tpu_custom_call", output_to_operand_aliasing={{0}: (8, {}), {1}: (9, {}), {2}: (10, {}), {3}: (11, {}), {... | custom-call | flops 134217728 | bytes 2097152 | tf_op jit(solution)/shard_map/pallas_call | solution.py:226
  43.8 0.1 collective-permute-start.9
  43.9 2.0 %collective-permute-start.10 = (f32[1,512,256]{2,1,0:T(8,128)S(1)}, f32[1,512,256]{2,1,0:T(8,128)S(1)}, u32[]{:S(2)}, u32[]{:S(2)}) collective-permute-start(f32[1,512,256]{2,1,0:T(8,128)S(1)} %get-tuple-element.56), channel_id=1, source_target_pairs={{8,16},{16,8},{9,17},{17,9},{10,18},{18,10},{11,19},{19,11},{12,20... | collective-permute-start | bytes 1572872 | tf_op jit(solution)/shard_map/ppermute | solution.py:297
  45.9 3.6 %collective-permute-start.13 = (f32[1,512,256]{2,1,0:T(8,128)S(1)}, f32[1,512,256]{2,1,0:T(8,128)S(1)}, u32[]{:S(2)}, u32[]{:S(2)}) collective-permute-start(f32[1,512,256]{2,1,0:T(8,128)S(1)} %get-tuple-element.60), channel_id=1, source_target_pairs={{8,16},{16,8},{9,17},{17,9},{10,18},{18,10},{11,19},{19,11},{12,20... | collective-permute-start | bytes 1572872 | tf_op jit(solution)/shard_map/ppermute | solution.py:298
  49.4 3.3 %collective-permute-start.8 = (f32[1,512,256]{2,1,0:T(8,128)S(1)}, f32[1,512,256]{2,1,0:T(8,128)S(1)}, u32[]{:S(2)}, u32[]{:S(2)}) collective-permute-start(f32[1,512,256]{2,1,0:T(8,128)S(1)} %get-tuple-element.53), channel_id=1, source_target_pairs={{2,4},{4,2},{3,5},{5,3},{10,12},{12,10},{11,13},{13,11},{18,20},{2... | collective-permute-start | bytes 1572872 | tf_op jit(solution)/shard_map/ppermute | solution.py:300
  52.7 1.9 %collective-permute-done.10.arrived = f32[1,512,256]{2,1,0:T(8,128)S(1)} collective-permute-done((f32[1,512,256]{2,1,0:T(8,128)S(1)}, f32[1,512,256]{2,1,0:T(8,128)S(1)}, u32[]{:S(2)}, u32[]{:S(2)}) %collective-permute-start.10) | collective-permute-done | bytes 524320 | tf_op jit(solution)/shard_map/ppermute | solution.py:297
  54.7 0.0 collective-permute-done.9.core_in
  54.7 0.1 shard_map.84
  54.7 1.5 %collective-permute-start.11 = (f32[1,512,256]{2,1,0:T(8,128)S(1)}, f32[1,512,256]{2,1,0:T(8,128)S(1)}, u32[]{:S(2)}, u32[]{:S(2)}) collective-permute-start(f32[1,512,256]{2,1,0:T(8,128)S(1)} %get-tuple-element.58), channel_id=1, source_target_pairs={{0,1},{1,0},{2,3},{3,2},{4,5},{5,4},{6,7},{7,6},{8,9},{9,8},{10,11... | collective-permute-start | bytes 1572872 | tf_op jit(solution)/shard_map/ppermute | solution.py:302
  56.2 0.0 collective-permute-start.12
  56.2 4.1 %collective-permute-done.13.arrived = f32[1,512,256]{2,1,0:T(8,128)S(1)} collective-permute-done((f32[1,512,256]{2,1,0:T(8,128)S(1)}, f32[1,512,256]{2,1,0:T(8,128)S(1)}, u32[]{:S(2)}, u32[]{:S(2)}) %collective-permute-start.13) | collective-permute-done | bytes 524320 | tf_op jit(solution)/shard_map/ppermute | solution.py:298
  60.3 0.1 shard_map.87
  60.4 1.9 %collective-permute-start.14 = (f32[1,512,256]{2,1,0:T(8,128)S(1)}, f32[1,512,256]{2,1,0:T(8,128)S(1)}, u32[]{:S(2)}, u32[]{:S(2)}) collective-permute-start(f32[1,512,256]{2,1,0:T(8,128)S(1)} %get-tuple-element.62), channel_id=1, source_target_pairs={{1,2},{2,1},{3,4},{4,3},{5,6},{6,5},{9,10},{10,9},{11,12},{12,11},... | collective-permute-start | bytes 1572872 | tf_op jit(solution)/shard_map/ppermute | solution.py:305
  62.3 3.8 %collective-permute-start.15 = (f32[1,512,256]{2,1,0:T(8,128)S(1)}, f32[1,512,256]{2,1,0:T(8,128)S(1)}, u32[]{:S(2)}, u32[]{:S(2)}) collective-permute-start(f32[1,512,256]{2,1,0:T(8,128)S(1)} %get-tuple-element.63), channel_id=1, source_target_pairs={{8,16},{16,8},{9,17},{17,9},{10,18},{18,10},{11,19},{19,11},{12,20... | collective-permute-start | bytes 1572872 | tf_op jit(solution)/shard_map/ppermute | solution.py:306
  66.1 0.0 collective-permute-done.8.arrived
  66.1 0.1 shard_map.83.refs_0_
  66.2 8.7 %collective-permute-done.11.refs_1_ = f32[1,512,256]{2,1,0:T(8,128)S(1)} collective-permute-done((f32[1,512,256]{2,1,0:T(8,128)S(1)}, f32[1,512,256]{2,1,0:T(8,128)S(1)}, u32[]{:S(2)}, u32[]{:S(2)}) %collective-permute-start.11) | collective-permute-done | bytes 524320 | tf_op jit(solution)/shard_map/ppermute | solution.py:302
  74.8 0.1 shard_map.85.refs_0_
  74.9 0.0 copy-start
  74.9 0.0 copy-start.1
  74.9 0.0 collective-permute-done.12.refs_1_
  74.9 0.1 shard_map.86.refs_0_
  75.0 0.0 collective-permute-done.14.refs_1_
  75.0 0.1 shard_map.88.refs_0_
  75.1 0.0 collective-permute-done.15.refs_1_
  75.1 0.9 %copy-done = bf16[1,512,512]{2,1,0:T(8,128)(2,1)S(1)} copy-done((bf16[1,512,512]{2,1,0:T(8,128)(2,1)S(1)}, bf16[1,512,512]{2,1,0:T(8,128)(2,1)}, u32[]{:S(2)}) %copy-start) | copy-done | bytes 524312
  76.0 0.2 copy-done.1
  76.1 1.1 %shard_map.89 = bf16[2,512,256]{2,1,0:T(8,128)(2,1)} custom-call(bf16[1,512,512]{2,1,0:T(8,128)(2,1)S(1)} %copy-done, bf16[2,512,256]{2,1,0:T(8,128)(2,1)S(1)} %copy-done.1, f32[1,512,256]{2,1,0:T(8,128)S(1)} %shard_map.88.refs_0_, f32[1,512,256]{2,1,0:T(8,128)S(1)} %collective-permute-done.15.refs_1_, bf16[512,256]{1,0:T(8,128)(2,1)S(1)} %get-tuple-element.64.refs_2_), custom_call_target="tpu_custom_call" | custom-call | tf_op jit(solution)/shard_map/pallas_call | solution.py:261
Async XLA Ops:
  4.4 13.6 %collective-permute-start.1 = (f32[3,512,256]{2,1,0:T(8,128)S(1)}, f32[3,512,256]{2,1,0:T(8,128)S(1)}, u32[]{:S(2)}, u32[]{:S(2)}) collective-permute-start(f32[3,512,256]{2,1,0:T(8,128)S(1)} %get-tuple-element.35.refs_5_), channel_id=1, source_target_pairs={{0,8},{8,0},{16,24},{24,16},{1,9},{9,1},{17,25},{25,17},{2,10},{10... | collective-permute-start | bytes 4718600 | tf_op jit(solution)/shard_map/ppermute | solution.py:299
  6.9 11.1 %collective-permute-start.2 = (f32[1,512,256]{2,1,0:T(8,128)S(1)}, f32[1,512,256]{2,1,0:T(8,128)S(1)}, u32[]{:S(2)}, u32[]{:S(2)}) collective-permute-start(f32[1,512,256]{2,1,0:T(8,128)S(1)} %get-tuple-element.38), channel_id=1, source_target_pairs={{8,16},{16,8},{9,17},{17,9},{10,18},{18,10},{11,19},{19,11},{12,20... | collective-permute-start | bytes 1572872 | tf_op jit(solution)/shard_map/ppermute | solution.py:297
  8.9 14.4 %collective-permute-start.5 = (f32[1,512,256]{2,1,0:T(8,128)S(1)}, f32[1,512,256]{2,1,0:T(8,128)S(1)}, u32[]{:S(2)}, u32[]{:S(2)}) collective-permute-start(f32[1,512,256]{2,1,0:T(8,128)S(1)} %get-tuple-element.42), channel_id=1, source_target_pairs={{8,16},{16,8},{9,17},{17,9},{10,18},{18,10},{11,19},{19,11},{12,20... | collective-permute-start | bytes 1572872 | tf_op jit(solution)/shard_map/ppermute | solution.py:298
  16.1 17.5 %collective-permute-start = (f32[1,512,256]{2,1,0:T(8,128)S(1)}, f32[1,512,256]{2,1,0:T(8,128)S(1)}, u32[]{:S(2)}, u32[]{:S(2)}) collective-permute-start(f32[1,512,256]{2,1,0:T(8,128)S(1)} %get-tuple-element.36), channel_id=1, source_target_pairs={{2,4},{4,2},{3,5},{5,3},{10,12},{12,10},{11,13},{13,11},{18,20},{2... | collective-permute-start | bytes 1572872 | tf_op jit(solution)/shard_map/ppermute | solution.py:300
  18.1 23.9 %collective-permute-start.3 = (f32[1,512,256]{2,1,0:T(8,128)S(1)}, f32[1,512,256]{2,1,0:T(8,128)S(1)}, u32[]{:S(2)}, u32[]{:S(2)}) collective-permute-start(f32[1,512,256]{2,1,0:T(8,128)S(1)} %get-tuple-element.40), channel_id=1, source_target_pairs={{0,1},{1,0},{2,3},{3,2},{4,5},{5,4},{6,7},{7,6},{8,9},{9,8},{10,11... | collective-permute-start | bytes 1572872 | tf_op jit(solution)/shard_map/ppermute | solution.py:302
  19.3 22.7 %collective-permute-start.4 = (f32[1,512,256]{2,1,0:T(8,128)S(1)}, f32[1,512,256]{2,1,0:T(8,128)S(1)}, u32[]{:S(2)}, u32[]{:S(2)}) collective-permute-start(f32[1,512,256]{2,1,0:T(8,128)S(1)} %get-tuple-element.41), channel_id=1, source_target_pairs={{0,2},{2,0},{1,3},{3,1},{4,6},{6,4},{5,7},{7,5},{8,10},{10,8},{9,1... | collective-permute-start | bytes 1572872 | tf_op jit(solution)/shard_map/ppermute | solution.py:303
  23.4 18.7 %collective-permute-start.6 = (f32[1,512,256]{2,1,0:T(8,128)S(1)}, f32[1,512,256]{2,1,0:T(8,128)S(1)}, u32[]{:S(2)}, u32[]{:S(2)}) collective-permute-start(f32[1,512,256]{2,1,0:T(8,128)S(1)} %get-tuple-element.44), channel_id=1, source_target_pairs={{1,2},{2,1},{3,4},{4,3},{5,6},{6,5},{9,10},{10,9},{11,12},{12,11},... | collective-permute-start | bytes 1572872 | tf_op jit(solution)/shard_map/ppermute | solution.py:305
  25.7 16.5 %collective-permute-start.7 = (f32[1,512,256]{2,1,0:T(8,128)S(1)}, f32[1,512,256]{2,1,0:T(8,128)S(1)}, u32[]{:S(2)}, u32[]{:S(2)}) collective-permute-start(f32[1,512,256]{2,1,0:T(8,128)S(1)} %get-tuple-element.45), channel_id=1, source_target_pairs={{8,16},{16,8},{9,17},{17,9},{10,18},{18,10},{11,19},{19,11},{12,20... | collective-permute-start | bytes 1572872 | tf_op jit(solution)/shard_map/ppermute | solution.py:306
  43.8 10.9 %collective-permute-start.9 = (f32[3,512,256]{2,1,0:T(8,128)S(1)}, f32[3,512,256]{2,1,0:T(8,128)S(1)}, u32[]{:S(2)}, u32[]{:S(2)}) collective-permute-start(f32[3,512,256]{2,1,0:T(8,128)S(1)} %get-tuple-element.54), channel_id=1, source_target_pairs={{0,8},{8,0},{16,24},{24,16},{1,9},{9,1},{17,25},{25,17},{2,10},{10... | collective-permute-start | bytes 4718600 | tf_op jit(solution)/shard_map/ppermute | solution.py:299
  43.9 10.8 %collective-permute-start.10 = (f32[1,512,256]{2,1,0:T(8,128)S(1)}, f32[1,512,256]{2,1,0:T(8,128)S(1)}, u32[]{:S(2)}, u32[]{:S(2)}) collective-permute-start(f32[1,512,256]{2,1,0:T(8,128)S(1)} %get-tuple-element.56), channel_id=1, source_target_pairs={{8,16},{16,8},{9,17},{17,9},{10,18},{18,10},{11,19},{19,11},{12,20... | collective-permute-start | bytes 1572872 | tf_op jit(solution)/shard_map/ppermute | solution.py:297
  45.9 14.4 %collective-permute-start.13 = (f32[1,512,256]{2,1,0:T(8,128)S(1)}, f32[1,512,256]{2,1,0:T(8,128)S(1)}, u32[]{:S(2)}, u32[]{:S(2)}) collective-permute-start(f32[1,512,256]{2,1,0:T(8,128)S(1)} %get-tuple-element.60), channel_id=1, source_target_pairs={{8,16},{16,8},{9,17},{17,9},{10,18},{18,10},{11,19},{19,11},{12,20... | collective-permute-start | bytes 1572872 | tf_op jit(solution)/shard_map/ppermute | solution.py:298
  49.4 16.6 %collective-permute-start.8 = (f32[1,512,256]{2,1,0:T(8,128)S(1)}, f32[1,512,256]{2,1,0:T(8,128)S(1)}, u32[]{:S(2)}, u32[]{:S(2)}) collective-permute-start(f32[1,512,256]{2,1,0:T(8,128)S(1)} %get-tuple-element.53), channel_id=1, source_target_pairs={{2,4},{4,2},{3,5},{5,3},{10,12},{12,10},{11,13},{13,11},{18,20},{2... | collective-permute-start | bytes 1572872 | tf_op jit(solution)/shard_map/ppermute | solution.py:300
  54.7 20.1 %collective-permute-start.11 = (f32[1,512,256]{2,1,0:T(8,128)S(1)}, f32[1,512,256]{2,1,0:T(8,128)S(1)}, u32[]{:S(2)}, u32[]{:S(2)}) collective-permute-start(f32[1,512,256]{2,1,0:T(8,128)S(1)} %get-tuple-element.58), channel_id=1, source_target_pairs={{0,1},{1,0},{2,3},{3,2},{4,5},{5,4},{6,7},{7,6},{8,9},{9,8},{10,11... | collective-permute-start | bytes 1572872 | tf_op jit(solution)/shard_map/ppermute | solution.py:302
  56.2 18.7 %collective-permute-start.12 = (f32[1,512,256]{2,1,0:T(8,128)S(1)}, f32[1,512,256]{2,1,0:T(8,128)S(1)}, u32[]{:S(2)}, u32[]{:S(2)}) collective-permute-start(f32[1,512,256]{2,1,0:T(8,128)S(1)} %get-tuple-element.59), channel_id=1, source_target_pairs={{0,2},{2,0},{1,3},{3,1},{4,6},{6,4},{5,7},{7,5},{8,10},{10,8},{9,1... | collective-permute-start | bytes 1572872 | tf_op jit(solution)/shard_map/ppermute | solution.py:303
  60.4 14.7 %collective-permute-start.14 = (f32[1,512,256]{2,1,0:T(8,128)S(1)}, f32[1,512,256]{2,1,0:T(8,128)S(1)}, u32[]{:S(2)}, u32[]{:S(2)}) collective-permute-start(f32[1,512,256]{2,1,0:T(8,128)S(1)} %get-tuple-element.62), channel_id=1, source_target_pairs={{1,2},{2,1},{3,4},{4,3},{5,6},{6,5},{9,10},{10,9},{11,12},{12,11},... | collective-permute-start | bytes 1572872 | tf_op jit(solution)/shard_map/ppermute | solution.py:305
  62.3 12.8 %collective-permute-start.15 = (f32[1,512,256]{2,1,0:T(8,128)S(1)}, f32[1,512,256]{2,1,0:T(8,128)S(1)}, u32[]{:S(2)}, u32[]{:S(2)}) collective-permute-start(f32[1,512,256]{2,1,0:T(8,128)S(1)} %get-tuple-element.63), channel_id=1, source_target_pairs={{8,16},{16,8},{9,17},{17,9},{10,18},{18,10},{11,19},{19,11},{12,20... | collective-permute-start | bytes 1572872 | tf_op jit(solution)/shard_map/ppermute | solution.py:306
  74.9 1.0 %copy-start = (bf16[1,512,512]{2,1,0:T(8,128)(2,1)S(1)}, bf16[1,512,512]{2,1,0:T(8,128)(2,1)}, u32[]{:S(2)}) copy-start(bf16[1,512,512]{2,1,0:T(8,128)(2,1)} %inverse.1) | copy-start | bytes 1572868
  74.9 1.2 %copy-start.1 = (bf16[2,512,256]{2,1,0:T(8,128)(2,1)S(1)}, bf16[2,512,256]{2,1,0:T(8,128)(2,1)}, u32[]{:S(2)}) copy-start(bf16[2,512,256]{2,1,0:T(8,128)(2,1)} %incident.1) | copy-start | bytes 1572868
